TPU v7x, 32 devices: a whole 2x2x4 slice. The times are simulated.
32 devices in a mesh: depth: 4 (over y, x), view: 8 (over z, core).
Axes of the slice: x: 2, y: 2, z: 4, core: 2. Of those that a mesh axis runs over, the one named last changes fastest.
Arguments:
- bricks: float32 [4, 8, 8, 64, 4096], P('depth', 'view'), may hold values from -6 to 6
- tile_holder: int32 [4, 8, 8], P('depth', 'view'), may hold values from -1 to 7, as said below
Outputs:
- image: float32 [4, 64, 4096], P(None, 'depth', 'view')
Inputs may be any that keep to these rules, and one draw needn't show every extreme that they name: Renderer (d, v) finds brick column t in slot t of holder tile_holder[d, v, t]. For fixed d and t the holders that appear are distinct over v, and the holders named by one renderer are distinct; brick column 0 is never skipped.
All inputs are finite; a program needn't handle non-finite values.
Results may differ from a plain program's by a relative error of at most 0.0003.
Values sent between devices are 32-bit elements; how exact they have to be, the bound alone decides.
No kernel may reach another device: no remote copies, remote signals or barrier semaphores. Data moves between devices by JAX's collectives and lax.ppermute only.
A program may use at most 128 MiB of HBM per device.

v0:
```python
import jax
import jax.numpy as jnp
from jax import lax
from jax.sharding import PartitionSpec as P

STEPS = 48


DENSITY = 0.8
ISO_LEVEL = 1.0
SHARPEN = 1.5


def partner(x, axis, stride):
    return lax.ppermute(x, axis, [(i, i ^ 1 << stride) for i in range(lax.axis_size(axis))])


def padded_2(x, sides, width):
    for axis, dim in sides:
        size, length = (lax.axis_size(axis), x.shape[dim])
        up = [(i, (i + 1) % size) for i in range(size - 1)]
        down = [(j, i) for i, j in up]
        last = lax.slice_in_dim(x, length - width, length, axis=dim)
        initial = lax.slice_in_dim(x, 0, width, axis=dim)
        before = lax.ppermute(last, axis, up)
        after = lax.ppermute(initial, axis, down)
        x = jnp.concatenate([before, x, after], axis=dim)
    return x


def sample_table(edge, count):
    spots = (jnp.arange(count, dtype=jnp.float32) + 0.5) * (edge / count) - 0.5
    spots = jnp.clip(spots, 0.0, edge - 1.0)
    voxels = jnp.arange(edge, dtype=jnp.float32)
    return jnp.maximum(0.0, 1.0 - jnp.abs(spots[:, None] - voxels[None, :]))


def prefix_table(count):
    steps_idx = jnp.arange(count, dtype=jnp.int32)
    return (steps_idx[:, None] > steps_idx[None, :]).astype(jnp.float32)


def neighbor_diff(values, edge):
    flat_idx = jnp.arange(edge * edge, dtype=jnp.int32)
    column = flat_idx % edge
    rowpos = flat_idx // edge
    right = jnp.where(column == edge - 1, values, jnp.roll(values, -1, axis=1))
    left = jnp.where(column == 0, values, jnp.roll(values, 1, axis=1))
    below = jnp.where(rowpos == edge - 1, values, jnp.roll(values, -edge, axis=1))
    above = jnp.where(rowpos == 0, values, jnp.roll(values, edge, axis=1))
    ahead = jnp.concatenate([values[1:], values[-1:]], axis=0)
    behind = jnp.concatenate([values[:1], values[:-1]], axis=0)
    return (right - left, below - above, ahead - behind)


def march_brick(brick, table, prefix):
    count = table.shape[0]
    edge = table.shape[1]
    samples = jnp.dot(table, brick, precision=lax.Precision.HIGHEST)
    grad_x, grad_y, grad_z = neighbor_diff(samples, edge)
    shade = 0.3 + 0.7 * jnp.abs(grad_z) / jnp.sqrt(
        grad_x * grad_x + grad_y * grad_y + grad_z * grad_z + 1.0
    )
    thickness = DENSITY / count * jax.nn.sigmoid(4.0 * (samples - ISO_LEVEL))
    optical = jnp.dot(prefix, thickness, precision=lax.Precision.HIGHEST)
    weight = jnp.exp(-optical) * (1.0 - jnp.exp(-thickness))
    lit = weight * shade
    red_sum = jnp.sum(lit * jax.nn.sigmoid(1.5 * samples), axis=0)
    green_sum = jnp.sum(lit * jax.nn.sigmoid(-1.5 * samples), axis=0)
    blue_sum = jnp.sum(lit * jax.nn.sigmoid(3.0 * (samples - 1.0)), axis=0)
    opacity = jnp.sum(weight, axis=0)
    return jnp.stack([red_sum, green_sum, blue_sum, opacity], axis=0)


def composite_over(front, back, axis):
    front_alpha = lax.slice_in_dim(front, 3, 4, axis=axis)
    return front + (1.0 - front_alpha) * back


def body(bricks, tile_holder):
    views = lax.axis_size("view")
    depths = lax.axis_size("depth")
    stored = bricks[0, 0]
    holders = tile_holder[0, 0]
    columns = stored.shape[0]
    edge = stored.shape[1]
    table = sample_table(edge, STEPS)
    prefix = prefix_table(STEPS)
    matches = holders[:, None] == jnp.arange(views, dtype=jnp.int32)[None, :]
    column_ids = jnp.arange(columns, dtype=jnp.int32)[:, None]
    wanted = jnp.max(jnp.where(matches, column_ids, -1), axis=0)
    asked = lax.all_to_all(
        wanted.reshape(views, 1), "view", split_axis=0, concat_axis=0, tiled=True
    ).reshape(views)
    slot_index = jnp.clip(asked, 0, columns - 1)
    source = jnp.clip(holders, 0, views - 1)
    visible = (holders >= 0).astype(jnp.float32)
    outgoing = stored[slot_index]
    arrived = lax.all_to_all(outgoing, "view", split_axis=0, concat_axis=0, tiled=True)
    tiles = lax.map(lambda index_one: march_brick(arrived[index_one], table, prefix), source)
    tiles = tiles * visible[:, None, None]
    region_cols = columns * edge
    region = (
        tiles.reshape(columns, 4, edge, edge).transpose(1, 2, 0, 3).reshape(4, edge * region_cols)
    )
    band = edge * region_cols // depths
    pieces = region.reshape(4, depths, band).transpose(1, 0, 2)
    depth_rank = lax.axis_index("depth")
    current = pieces
    for level in range(depths.bit_length() - 1):
        halves = current.reshape(current.shape[0] // 2, 2, 4, band)
        my_bit = depth_rank // 2**level % 2
        kept = lax.dynamic_index_in_dim(halves, my_bit, 1, keepdims=False)
        given = lax.dynamic_index_in_dim(halves, 1 - my_bit, 1, keepdims=False)
        received = partner(given, "depth", level)
        current = jnp.where(
            my_bit == 0, composite_over(kept, received, 1), composite_over(received, kept, 1)
        )
    merged = current[0]
    band_rows = edge // depths
    block = merged.reshape(4, band_rows, region_cols)
    padded = padded_2(block, (("depth", 1), ("view", 2)), 1)
    rows_done = 0.25 * padded[:, :-2] + 0.5 * padded[:, 1:-1] + 0.25 * padded[:, 2:]
    blurred = 0.25 * rows_done[:, :, :-2] + 0.5 * rows_done[:, :, 1:-1] + 0.25 * rows_done[:, :, 2:]
    return block + SHARPEN * (block - blurred)


def solution(mesh):
    in_specs = (P("depth", "view", None, None, None), P("depth", "view", None))
    out_specs = P(None, "depth", "view")
    return jax.shard_map(body, mesh=mesh, in_specs=in_specs, out_specs=out_specs, check_vma=False)
```

profile of v0, /device:TPU:0, one launch (start us, length us, event | category | flops | bytes accessed | tf_op | source)
XLA Modules:
  0.0 304.9 jit_solution(2238676087967871938)
XLA Ops:
  0.8 11.7 %all_to_all.14 = s32[8,1,1]{2,1,0:T(1,128)S(1)} all-to-all(s32[8,1,1]{2,1,0:T(1,128)S(1)} %copy.11), channel_id=1, replica_groups=mesh['depth'=4,'view'=8] {'view'}, dimensions={0} | all-to-all | bytes 64 | tf_op jit(solution)/shard_map/all_to_all | solution.py:92
  12.8 7.7 %gather_fusion = f32[8,64,4096]{2,1,0:T(8,128)} fusion(f32[8,64,4096]{2,1,0:T(8,128)} %bitcast.69, s32[1024]{0:T(1024)S(1)} %pad_clamp_fusion), kind=kCustom, calls=%fused_computation | custom fusion | bytes 16777248 | tf_op jit(solution)/shard_map/gather | solution.py:98
  20.4 5.1 %all-to-all-start.1 = ((f32[8,64,4096]{2,1,0:T(8,128)}), f32[8,64,4096]{2,1,0:T(8,128)}, u32[]{:S(2)}, u32[]{:S(2)}) async-start(f32[8,64,4096]{2,1,0:T(8,128)} %gather_fusion), calls=%async_computation.1 | async-start | bytes 16777216 | tf_op jit(solution)/shard_map/all_to_all | solution.py:99
  25.7 183.8 %all-to-all-done.1 = f32[8,64,4096]{2,1,0:T(8,128)} async-done(((f32[8,64,4096]{2,1,0:T(8,128)}), f32[8,64,4096]{2,1,0:T(8,128)}, u32[]{:S(2)}, u32[]{:S(2)}) %all-to-all-start.1) | async-done | bytes 8388640 | tf_op jit(solution)/shard_map/all_to_all | solution.py:99
  209.4 65.4 %while.13 = (s32[]{:T(128)}, f32[8,4,4096]{2,1,0:T(4,128)S(1)}, s32[8]{0:T(128)S(1)}, f32[8,64,4096]{2,1,0:T(8,128)}, f32[48]{0:T(128)S(1)}, /*index=5*/s32[]{:T(128)}, s32[]{:T(128)}, s32[]{:T(128)}) while((s32[]{:T(128)}, f32[8,4,4096]{2,1,0:T(4,128)S(1)}, s32[8]{0:T(128)S(1)}, f32[8,64,4096]{2,1,0:T(8,128)}, f32[48]{0:T(128)S(1)}, ...), condition=%wide.region_6.7_spmd.clone, body=%wide.region_1.6_spmd.clone.sunk | while | flops 276161024 | bytes 19366220 | solution.py:100
  211.9 2.1 convolution_bitcast_fusion.2
  214.9 1.9 fusion.94
  220.1 2.1 convolution_bitcast_fusion.2
  223.1 1.9 fusion.94
  228.3 2.1 convolution_bitcast_fusion.2
  231.3 1.9 fusion.94
  236.4 2.1 convolution_bitcast_fusion.2
  239.4 1.9 fusion.94
  244.6 2.1 convolution_bitcast_fusion.2
  252.8 2.1 convolution_bitcast_fusion.2
  255.8 1.9 fusion.94
  261.0 2.1 convolution_bitcast_fusion.2
  264.0 1.9 fusion.94
  269.2 2.1 convolution_bitcast_fusion.2
  272.1 1.9 fusion.94
  278.7 6.2 %collective-permute-done = f32[2,4,8192]{2,1,0:T(4,128)S(1)} collective-permute-done((f32[2,4,8192]{2,1,0:T(4,128)S(1)}, f32[2,4,8192]{2,1,0:T(4,128)S(1)}, u32[]{:S(2)}, u32[]{:S(2)}) %collective-permute-start) | collective-permute-done | bytes 262176 | tf_op jit(solution)/shard_map/ppermute | solution.py:15
  286.8 3.4 %collective-permute-done.1 = f32[1,4,8192]{2,1,0:T(4,128)S(1)} collective-permute-done((f32[1,4,8192]{2,1,0:T(4,128)S(1)}, f32[1,4,8192]{2,1,0:T(4,128)S(1)}, u32[]{:S(2)}, u32[]{:S(2)}) %collective-permute-start.1) | collective-permute-done | bytes 131104 | tf_op jit(solution)/shard_map/ppermute | solution.py:15
  290.4 3.4 %collective-permute-start.2 = (f32[4,1,512]{2,1,0:T(1,128)S(1)}, f32[4,1,512]{2,1,0:T(1,128)S(1)}, u32[]{:S(2)}, u32[]{:S(2)}) collective-permute-start(f32[4,1,512]{2,1,0:T(1,128)S(1)} %get-tuple-element.137), channel_id=1, source_target_pairs={{0,8},{8,16},{16,24},{1,9},{9,17},{17,25},{2,10},{10,18},{18,26},{... | collective-permute-start | bytes 24584 | tf_op jit(solution)/shard_map/ppermute | solution.py:25
  295.2 4.2 %collective-permute-done.3 = f32[4,1,512]{2,1,0:T(1,128)S(1)} collective-permute-done((f32[4,1,512]{2,1,0:T(1,128)S(1)}, f32[4,1,512]{2,1,0:T(1,128)S(1)}, u32[]{:S(2)}, u32[]{:S(2)}) %collective-permute-start.3) | collective-permute-done | bytes 8224 | tf_op jit(solution)/shard_map/ppermute | solution.py:26
  (129 shorter events, 34.0 us)
Async XLA Ops:
  20.4 5.2 %copy-start = (s32[1,1,8]{2,1,0:T(1,128)S(1)}, s32[1,1,8]{2,1,0:T(1,128)}, u32[]{:S(2)}) copy-start(s32[1,1,8]{2,1,0:T(1,128)} %param.5) | copy-start | bytes 100
  20.4 189.0 %all-to-all-start.1 = ((f32[8,64,4096]{2,1,0:T(8,128)}), f32[8,64,4096]{2,1,0:T(8,128)}, u32[]{:S(2)}, u32[]{:S(2)}) async-start(f32[8,64,4096]{2,1,0:T(8,128)} %gather_fusion), calls=%async_computation.1 | async-start | bytes 16777216 | tf_op jit(solution)/shard_map/all_to_all | solution.py:99
  277.0 7.9 %collective-permute-start = (f32[2,4,8192]{2,1,0:T(4,128)S(1)}, f32[2,4,8192]{2,1,0:T(4,128)S(1)}, u32[]{:S(2)}, u32[]{:S(2)}) collective-permute-start(f32[2,4,8192]{2,1,0:T(4,128)S(1)} %get-tuple-element.134), channel_id=1, source_target_pairs={{0,8},{8,0},{16,24},{24,16},{1,9},{9,1},{17,25},{25,17},{2,10},{10... | collective-permute-start | bytes 786440 | tf_op jit(solution)/shard_map/ppermute | solution.py:15
  285.2 5.0 %collective-permute-start.1 = (f32[1,4,8192]{2,1,0:T(4,128)S(1)}, f32[1,4,8192]{2,1,0:T(4,128)S(1)}, u32[]{:S(2)}, u32[]{:S(2)}) collective-permute-start(f32[1,4,8192]{2,1,0:T(4,128)S(1)} %constant_dynamic-slice_fusion), channel_id=1, source_target_pairs={{0,16},{8,24},{16,0},{24,8},{1,17},{9,25},{17,1},{25,9},{2,18},{10... | collective-permute-start | bytes 393224 | tf_op jit(solution)/shard_map/ppermute | solution.py:15
  290.4 4.7 %collective-permute-start.2 = (f32[4,1,512]{2,1,0:T(1,128)S(1)}, f32[4,1,512]{2,1,0:T(1,128)S(1)}, u32[]{:S(2)}, u32[]{:S(2)}) collective-permute-start(f32[4,1,512]{2,1,0:T(1,128)S(1)} %get-tuple-element.137), channel_id=1, source_target_pairs={{0,8},{8,16},{16,24},{1,9},{9,17},{17,25},{2,10},{10,18},{18,26},{... | collective-permute-start | bytes 24584 | tf_op jit(solution)/shard_map/ppermute | solution.py:25
  293.8 5.5 %collective-permute-start.3 = (f32[4,1,512]{2,1,0:T(1,128)S(1)}, f32[4,1,512]{2,1,0:T(1,128)S(1)}, u32[]{:S(2)}, u32[]{:S(2)}) collective-permute-start(f32[4,1,512]{2,1,0:T(1,128)S(1)} %get-tuple-element.138), channel_id=1, source_target_pairs={{8,0},{16,8},{24,16},{9,1},{17,9},{25,17},{10,2},{18,10},{26,18},{... | collective-permute-start | bytes 24584 | tf_op jit(solution)/shard_map/ppermute | solution.py:26
  299.4 2.6 collective-permute-start.4
  300.7 3.1 %collective-permute-start.5 = (f32[4,18,1]{2,1,0:T(8,128)S(1)}, f32[4,18,1]{2,1,0:T(8,128)S(1)}, u32[]{:S(2)}, u32[]{:S(2)}) collective-permute-start(f32[4,18,1]{2,1,0:T(8,128)S(1)} %get-tuple-element.136), channel_id=1, source_target_pairs={{1,0},{2,1},{3,2},{4,3},{5,4},{6,5},{7,6},{9,8},{10,9},{11,10},{12... | collective-permute-start | bytes 872 | tf_op jit(solution)/shard_map/ppermute | solution.py:26
where the time goes:
time: 308 us; the launch traced here: 305 us
  waiting for transfers between devices  199 us (65%)
  matrix products  31.7 us (10%)
  local copies, waits for them, and re-layouts  21.8 us (7%)
  starting transfers between devices  15.5 us (5%)
  loops' own time  15.5 us (5%)
  blocking collectives  11.7 us (4%)
  other arithmetic  9.14 us (3%)
    all_to_all x1, waiting for transfers between devices, body(): lax.all_to_all(outgoing, 'view', split_axis=0, concat_axis=0, tiled=True)  184 us
    dot_general x8, matrix products, march_brick(): samples = jnp.dot(table, brick, precision=lax.Precision.HIGHEST)  16.7 us
    another operation x1, loops' own time, body(): lax.map(lambda index_one: march_brick(arrived[index_one], table, prefix),...  15.5 us
    dot_general x8, matrix products, march_brick(): optical = jnp.dot(prefix, thickness, precision=lax.Precision.HIGHEST)  14.9 us
    all_to_all x1, blocking collectives, body(): lax.all_to_all(wanted.reshape(views, 1), 'view', split_axis=0, concat_axi...  11.7 us
    ppermute x2, waiting for transfers between devices, partner(): lax.ppermute(x, axis, [(i, i ^ 1 << stride) for i in range(lax.axis_size(...  9.61 us
    gather x1, local copies, waits for them, and re-layouts, body(): outgoing = stored[slot_index]  7.68 us
  transfers between devices with their start and end apart: 7, of which 5 were waited for; matrix products, arithmetic and copies ran while one was open for 0% of the time, Pallas kernels for 0%

commit v1 on v0

v1 whole, which is shorter than its diff:
```python
import functools

import jax
import jax.numpy as jnp
from jax import lax
from jax.experimental import pallas as pl
from jax.experimental.pallas import tpu as pltpu
from jax.sharding import PartitionSpec as P

STEPS = 48
DENSITY = 0.8
SHARPEN = 1.5
LANES = 128
PHASES = 2


class Plan:
    def __init__(self, depths, views, columns, edge, area):
        self.depths, self.views, self.columns = depths, views, columns
        self.edge, self.area = edge, area
        self.pairs = area // LANES
        self.band = self.pairs // depths
        self.half = self.band // PHASES
        self.rows = 4 * self.half + 4
        self.blocks = -(-self.rows // 8)
        self.tiles = columns * depths
        self.slots = max(1, 8 // depths)
        self.subs = max(1, depths // 8)
        self.groups = columns // self.slots
        self.peers = depths * views
        self.zts = edge // 8


def roll(x, shift, axis=1):
    return pltpu.roll(x, shift % x.shape[axis], axis)


def lane_of(shape):
    return lax.broadcasted_iota(jnp.int32, shape, 1)


def march_group(plan, phase, load, top, bottom):
    half = plan.half
    scale = DENSITY / (2 * STEPS)
    lane = lane_of((8, LANES))
    low = lane < 64
    inside = (lane % 64 != 0).astype(jnp.float32)

    def three(zt, part):
        planes = [[load(zt, 4 * part + r, a) for a in range(half + 2)] for r in range(4)]
        first = [5.0 * p + q for p, q in zip(planes[0], planes[1])]
        second = [3.0 * (p + q) for p, q in zip(planes[1], planes[2])]
        third = [p + 5.0 * q for p, q in zip(planes[2], planes[3])]
        return [first, second, third]

    def step(index, behind, here, ahead, carry):
        body = here[1 : half + 1]
        turned = [roll(x, 64) for x in here]
        if phase == 0:
            turned[0] = jnp.where(top, body[0], turned[0])
        if phase == PHASES - 1:
            turned[-1] = jnp.where(bottom, body[-1], turned[-1])
        steps_y = [turned[i + 1] - turned[i] for i in range(half + 1)]
        out = []
        for a in range(half):
            total, trans, lit, red, blue = carry[a]
            x = body[a]
            grad_y = jnp.where(low, steps_y[a], steps_y[a + 1])
            diff = (x - roll(x, 1)) * inside
            grad_x = diff + roll(diff, -1)
            grad_z = ahead[a + 1] - behind[a + 1]
            norm = grad_x * grad_x + grad_y * grad_y + (grad_z * grad_z + 36.0)
            slope = jnp.abs(grad_z) * lax.rsqrt(norm)
            total = total + jnp.tanh(x * (1.0 / 3.0) - 2.0)
            later = jnp.exp(total * -scale - scale * (index + 1))
            part = (trans - later) * (slope + 3.0 / 7.0)
            out.append(
                (
                    total,
                    later,
                    lit + part,
                    red + part * jnp.tanh(x * 0.125),
                    blue + part * jnp.tanh(x * 0.25 - 1.5),
                )
            )
        return out

    zero = jnp.zeros((8, LANES), jnp.float32)
    carry = [(zero, zero + 1.0, zero, zero, zero)] * half
    window = []
    count = 0
    for zt in range(plan.zts):
        for part in range(2):
            for sample in three(zt, part):
                window.append(sample)
                if len(window) == 1:
                    window.append(sample)
                    window = [sample, sample]
                    continue
                if len(window) == 3:
                    carry = step(count, window[0], window[1], window[2], carry)
                    count += 1
                    window = window[1:]
    carry = step(count, window[0], window[1], window[1], carry)
    value = [[], [], [], []]
    for _, trans, lit, red, blue in carry:
        value[0].append(0.35 * (lit + red))
        value[1].append(0.35 * (lit - red))
        value[2].append(0.35 * (lit + blue))
        value[3].append(1.0 - trans)
    return value


def store_tiles(plan, phase, value, tiles_ref, base, first_slot):
    half = plan.half
    lane = lane_of((8, LANES))
    low = lane < 64
    rows = [value[c][a] for c in range(4) for a in range(half)]
    for c in (0, 2):
        if phase == 0:
            x, y = value[c][0], value[c + 1][0]
            rows.append(jnp.where(low, x, roll(y, 64)))
        else:
            x, y = value[c][-1], value[c + 1][-1]
            rows.append(jnp.where(low, roll(x, 64), y))
    first = jnp.zeros((8, LANES), jnp.float32)
    last = first
    for c in range(4):
        for a in range(half):
            spot = 4 * a + c
            first += roll(jnp.where(lane % 64 == 0, value[c][a], 0.0), spot)
            last += roll(jnp.where(lane % 64 == 63, value[c][a], 0.0), 4 * half + spot - 63)
    rim = jnp.where(first_slot, first, last)
    rows += [rim, rim]
    for i, row in enumerate(rows):
        start = ((i // 8) * plan.tiles + base) * 8 + i % 8
        tiles_ref[pl.ds(start, 8, 8), :] = row


def assemble(plan, phase, tiles_ref, route_ref, me_ref, out_ref):
    depths, views, half = plan.depths, plan.views, plan.half
    mine = me_ref[0]
    row = lax.broadcasted_iota(jnp.int32, (4, LANES), 0)
    zero = jnp.zeros((4, LANES), jnp.float32)

    def piece(slot, band, index):
        at = ((4 * index // 8) * plan.tiles + slot * depths + band) * 8 + 4 * index % 8
        return tiles_ref[pl.ds(at, 4), :]

    asked = [route_ref[mine * views + v, 0] for v in range(views)]
    for v in range(views):
        slot = jnp.maximum(asked[v], 0)
        right = left = None
        if v + 1 < views:
            right = jnp.where(asked[v + 1] == 0, 1.0, 0.0)
        if v > 0:
            left = jnp.where(asked[v - 1] == plan.columns - 1, 1.0, 0.0)

        def rim(band):
            total = zero
            if right is not None:
                total = total + right * piece(0, band, half)
            if left is not None:
                total = total + left * piece(plan.columns - 1, band, half)
            return total

        for band in range(depths):
            at = (band * views + v) * plan.rows
            for index in range(half):
                out_ref[pl.ds(at + 4 * index, 4), :] = piece(slot, band, index)
            near = band + 1 if phase == 0 else band - 1
            exists = 0 <= near < depths
            outer = piece(slot, near, half) if exists else zero
            corner = rim(near) if exists else zero
            tail = jnp.where(row < 2, outer, jnp.where(row == 2, rim(band), corner))
            out_ref[pl.ds(at + 4 * half, 4), :] = tail


def march_kernel(plan, phase, joined, *refs):
    if joined:
        route_ref, me_ref, x_ref, out_ref, tiles_ref, held, sems = refs
    else:
        x_ref, tiles_ref, held, sems = refs
    step = pl.program_id(0)
    half, depths = plan.half, plan.depths
    wide = min(depths, 8)

    def copies(group, parity):
        result = []
        for sub in range(plan.subs):
            for slot in range(plan.slots):
                for a in range(half + 2):
                    at = half * phase - 1 + a
                    move = -1 if at < 0 else (1 if at >= plan.band else 0)
                    at = at % plan.band
                    begin = sub * 8 + move
                    end = min(begin + wide, depths)
                    start = max(begin, 0)
                    source = x_ref.at[group * plan.slots + slot, :, pl.ds(start, end - start), at]
                    target = held.at[
                        parity, sub, :, a, pl.ds(slot * wide + start - begin, end - start)
                    ]
                    result.append(
                        pltpu.make_async_copy(source, target, sems.at[parity, len(result)])
                    )
        return result

    @pl.when(step == 0)
    def _():
        for copy in copies(0, 0):
            copy.start()

    @pl.when(step + 1 < plan.groups)
    def _():
        for copy in copies(step + 1, (step + 1) % 2):
            copy.start()

    for copy in copies(step, step % 2):
        copy.wait()

    size = plan.zts * (half + 2) * 64
    flat = held.reshape(2 * plan.subs * size, LANES)
    sub_row = lax.broadcasted_iota(jnp.int32, (8, LANES), 0)
    for sub in range(plan.subs):
        origin = ((step % 2) * plan.subs + sub) * size

        def load(zt, r, a):
            return flat[pl.ds(origin + (zt * (half + 2) + a) * 64 + r, 8, 8), :]

        top = sub_row % wide == 0 if sub == 0 else None
        bottom = sub_row % wide == wide - 1 if sub == plan.subs - 1 else None
        never = sub_row < 0
        value = march_group(
            plan, phase, load, never if top is None else top, never if bottom is None else bottom
        )
        first_slot = step * plan.slots + sub_row // wide == 0
        base = step * plan.slots * depths + 8 * sub
        store_tiles(plan, phase, value, tiles_ref, base, first_slot)

    if joined:

        @pl.when(step == plan.groups - 1)
        def _():
            assemble(plan, phase, tiles_ref, route_ref, me_ref, out_ref)


SMEM = pl.BlockSpec(memory_space=pltpu.SMEM)


def march(plan, phase, bricks, route=None):
    joined = route is not None
    tiles = (plan.blocks * plan.tiles * 8, LANES)
    shape = (plan.peers * plan.rows, LANES) if joined else tiles
    copies = plan.subs * plan.slots * (plan.half + 2)
    held = (2, plan.subs, plan.zts, plan.half + 2, 8, 8, LANES)
    scratch = [pltpu.VMEM(tiles, jnp.float32)] if joined else []
    pixels = plan.columns * plan.area // PHASES
    return pl.pallas_call(
        functools.partial(march_kernel, plan, phase, joined),
        grid=(plan.groups,),
        in_specs=([SMEM, SMEM] if joined else []) + [pl.BlockSpec(memory_space=pl.ANY)],
        out_specs=pl.BlockSpec(shape, lambda i: (0, 0)),
        out_shape=jax.ShapeDtypeStruct(shape, jnp.float32),
        scratch_shapes=scratch
        + [pltpu.VMEM(held, jnp.float32), pltpu.SemaphoreType.DMA((2, copies))],
        cost_estimate=pl.CostEstimate(
            flops=40 * STEPS * pixels, bytes_accessed=6 * plan.edge * pixels, transcendentals=5 * STEPS * pixels
        ),
        name=f"march_{phase}",
    )(*(route if joined else ()), bricks)


def assemble_kernel(plan, phase, route_ref, me_ref, tiles_ref, out_ref):
    assemble(plan, phase, tiles_ref, route_ref, me_ref, out_ref)


def message(plan, phase, tiles, route):
    return pl.pallas_call(
        functools.partial(assemble_kernel, plan, phase),
        in_specs=[SMEM, SMEM, pl.BlockSpec(memory_space=pltpu.VMEM)],
        out_specs=pl.BlockSpec(memory_space=pltpu.VMEM),
        out_shape=jax.ShapeDtypeStruct((plan.peers * plan.rows, LANES), jnp.float32),
        name=f"message_{phase}",
    )(*route, tiles)


def finish_kernel(plan, route_ref, me_ref, near_ref, far_ref, out_ref, image):
    depths, views, half, band = plan.depths, plan.views, plan.half, plan.band
    columns = plan.columns
    lane = lane_of((1, LANES))
    low = lane < 64
    view = me_ref[1]
    sources = (near_ref, far_ref)
    side = 4 * half

    def over(front, alpha, back):
        return front if back is None else front + (1.0 - alpha) * back

    bodies, outers = [], []
    for t in range(columns):
        body, outer = [], []
        for ref in sources:
            acc, rim = [None] * 4, [None] * 2
            for d in reversed(range(depths)):
                holder = route_ref[d * views + view, 1 + t]
                shown = jnp.where(holder >= 0, 1.0, 0.0)
                at = (d * views + jnp.maximum(holder, 0)) * plan.rows
                front = [ref[pl.ds(at + c * half, half), :] * shown for c in range(4)]
                acc = [over(f, front[3], b) for f, b in zip(front, acc)]
                front = [ref[pl.ds(at + 4 * half + i, 1), :] * shown for i in range(2)]
                alpha = jnp.where(low, roll(front[1], 64), front[1])
                rim = [over(f, alpha, b) for f, b in zip(front, rim)]
            body.append(acc)
            outer.append(rim)
        bodies.append([jnp.concatenate([body[0][c], body[1][c]], axis=0) for c in range(4)])
        outers.append(outer)

    sides = []
    lane2 = lane_of((2, LANES))
    for ref in sources:
        acc = None
        for d in reversed(range(depths)):
            front = None
            for h in range(views):
                piece = ref[pl.ds((d * views + h) * plan.rows + 4 * half + 2, 2), :]
                front = piece if front is None else front + piece
            alpha = front
            for c in range(3):
                alpha = jnp.where(lane2 % 4 == c, roll(front, c - 3), alpha)
            acc = over(front, alpha, acc)
        sides.append(acc)

    count = 2 * band
    wide = lane_of((band, LANES))
    low_band = wide < 64
    number = lax.broadcasted_iota(jnp.int32, (band, LANES), 0) % half
    final = columns // 2 + 1
    spread = jnp.concatenate(
        [jnp.broadcast_to(s[0:1], (half, LANES)) for s in sides], axis=0
    )
    for c in range(4):
        for u in range(columns // 2):
            x, y = bodies[2 * u][c], bodies[2 * u + 1][c]
            image[c, u + 1, pl.ds(8, band, 2), :] = jnp.where(low_band, x, roll(y, 64))
            image[c, u + 1, pl.ds(9, band, 2), :] = jnp.where(low_band, roll(x, 64), y)
            for source, at in ((0, 8 + count), (1, 7)):
                x, y = outers[2 * u][source][c // 2], outers[2 * u + 1][source][c // 2]
                if c % 2 == 0:
                    y = roll(y, 64)
                else:
                    x = roll(x, 64)
                image[c, u + 1, pl.ds(at, 1), :] = jnp.where(low, x, y)
        for base, tile, spot in ((0, final, 0), (side, 0, LANES - 1)):
            for odd in range(2):
                here = wide == base + 64 * odd + 4 * number + c
                column = jnp.sum(jnp.where(here, spread, 0.0), axis=1, keepdims=True)
                image[c, tile, pl.ds(8 + odd, band, 2), :] = jnp.where(wide == spot, column, 0.0)
            for source, at, where in (
                (0, 8 + count, base + c),
                (1, 7, 64 + base + 4 * (half - 1) + c),
            ):
                corner = jnp.sum(
                    jnp.where(lane == where, sides[source][1:2], 0.0), axis=1, keepdims=True
                )
                image[c, tile, pl.ds(at, 1), :] = jnp.where(lane == spot, corner, 0.0)

    full = lane_of((count, LANES))
    for c in range(4):
        middle = [image[c, k, pl.ds(8, count), :] for k in range(final + 1)]
        smooth = [
            0.25 * image[c, k, pl.ds(7, count), :]
            + 0.5 * middle[k]
            + 0.25 * image[c, k, pl.ds(9, count), :]
            for k in range(final + 1)
        ]
        later = [roll(x, 1) for x in smooth]
        sooner = [roll(x, -1) for x in smooth]
        for k in range(1, final):
            left = jnp.where(full == 0, later[k - 1], later[k])
            right = jnp.where(full == LANES - 1, sooner[k + 1], sooner[k])
            blurred = 0.25 * left + 0.5 * smooth[k] + 0.25 * right
            out_ref[c, :, pl.ds((k - 1) * LANES, LANES)] = middle[k] + SHARPEN * (
                middle[k] - blurred
            )


def finish(plan, near, far, route):
    count = 2 * plan.band
    return pl.pallas_call(
        functools.partial(finish_kernel, plan),
        in_specs=[SMEM, SMEM] + [pl.BlockSpec(memory_space=pltpu.VMEM)] * 2,
        out_specs=pl.BlockSpec(memory_space=pltpu.VMEM),
        out_shape=jax.ShapeDtypeStruct((4, count, plan.columns * 64), jnp.float32),
        scratch_shapes=[
            pltpu.VMEM((4, plan.columns // 2 + 2, count + 16, LANES), jnp.float32)
        ],
        name="finish",
    )(*route, near, far)


def exchange(plan, messages):
    cut = messages.reshape(plan.peers, plan.rows // 4, 4, LANES)
    moved = lax.all_to_all(cut, ("depth", "view"), split_axis=0, concat_axis=0, tiled=True)
    return moved.reshape(plan.peers * plan.rows, LANES)


def body(bricks, tile_holder):
    depths, views = lax.axis_size("depth"), lax.axis_size("view")
    columns, edge, area = bricks.shape[2:]
    plan = Plan(depths, views, columns, edge, area)
    holders = tile_holder[0, 0]
    matches = holders[:, None] == jnp.arange(views, dtype=jnp.int32)[None, :]
    slots = jnp.arange(columns, dtype=jnp.int32)[:, None]
    wanted = jnp.max(jnp.where(matches, slots, -1), axis=0)
    request = jnp.concatenate(
        [wanted[:, None], jnp.broadcast_to(holders[None, :], (views, columns))], axis=1
    )
    request = jnp.broadcast_to(request[None], (depths, views, columns + 1))
    request = request.reshape(plan.peers, columns + 1)
    route = lax.all_to_all(request, ("depth", "view"), split_axis=0, concat_axis=0, tiled=True)
    me = jnp.stack([lax.axis_index("depth"), lax.axis_index("view")]).astype(jnp.int32)
    route = (route, me)
    stored = bricks[0, 0].reshape(columns, plan.zts, 8, plan.pairs, LANES).transpose(0, 1, 3, 2, 4)
    stored = stored.reshape(columns, plan.zts, depths, plan.band, 8, LANES)
    tiles = march(plan, 0, stored)
    near = exchange(plan, message(plan, 0, tiles, route))
    far = exchange(plan, march(plan, 1, stored, route))
    return finish(plan, near, far, route)


def solution(mesh):
    in_specs = (P("depth", "view", None, None, None), P("depth", "view", None))
    out_specs = P(None, "depth", "view")
    return jax.shard_map(body, mesh=mesh, in_specs=in_specs, out_specs=out_specs, check_vma=False)
```

time: 308 us -> 56.8 us (0.18)
  waiting for transfers between devices: 199 us -> 3.13 us
  matrix products: 31.7 us -> 0 us
  Pallas kernels: 0 us -> 21 us
  local copies, waits for them, and re-layouts: 21.8 us -> 2.02 us
  loops' own time: 15.5 us -> 0 us
  other arithmetic: 9.14 us -> 1.4 us
  blocking collectives: 11.7 us -> 15.4 us
    all_to_all x1 -> x2, waiting for transfers between devices: 184 us -> 3.13 us  [the longest x1 3.13 us: exchange(): lax.all_to_all(cut, ('depth', 'view'), split_axis=0, concat_axis=0, tiled...]
    dot_general x16 -> x0, matrix products: 31.7 us -> none  [the longest x8 16.7 us: march_brick(): samples = jnp.dot(table, brick, precision=lax.Precision.HIGHEST)]
    pallas_call x0 -> x4, Pallas kernels: none -> 21 us  [the longest x2 16.9 us: march(): pl.pallas_call(functools.partial(march_kernel, plan, phase, joined), grid...]
    ppermute x6 -> x0, waiting for transfers between devices: 15.7 us -> none  [the longest x2 9.61 us: partner(): lax.ppermute(x, axis, [(i, i ^ 1 << stride) for i in range(lax.axis_size(...]
    another operation x1 -> x0, loops' own time: 15.5 us -> none  [body(): lax.map(lambda index_one: march_brick(arrived[index_one], table, prefix),...]
    ppermute x6 -> x0, starting transfers between devices: 10.4 us -> none  [the longest x2 4.68 us: padded_2(): before = lax.ppermute(last, axis, up)]
    all_to_all x1 -> x2, starting transfers between devices: 5.08 us -> 13.1 us  [the longest x1 7.3 us: body(): lax.all_to_all(request, ('depth', 'view'), split_axis=0, concat_axis=0, t...]
    gather x1 -> x0, local copies, waits for them, and re-layouts: 7.68 us -> none  [body(): outgoing = stored[slot_index]]
  transfers between devices with their start and end apart: 7 -> 2, of which waited for: 5 -> 1; matrix products, arithmetic and copies ran while one was open for 0% -> 1% of each run, Pallas kernels for 0% -> 30%
where the time goes in v1:
time: 56.8 us; the launch traced here: 56.2 us
  Pallas kernels  21 us (37%)
  blocking collectives  15.4 us (27%)
  starting transfers between devices  13.1 us (23%)
  waiting for transfers between devices  3.13 us (6%)
  local copies, waits for them, and re-layouts  2.02 us (4%)
  other arithmetic  1.4 us (2%)
    pallas_call x2, Pallas kernels, march(): pl.pallas_call(functools.partial(march_kernel, plan, phase, joined), grid...  16.9 us
    all_to_all x1, blocking collectives, exchange(): lax.all_to_all(cut, ('depth', 'view'), split_axis=0, concat_axis=0, tiled...  15.4 us
    all_to_all x1, starting transfers between devices, body(): lax.all_to_all(request, ('depth', 'view'), split_axis=0, concat_axis=0, t...  7.3 us
    all_to_all x1, starting transfers between devices, exchange(): lax.all_to_all(cut, ('depth', 'view'), split_axis=0, concat_axis=0, tiled...  5.83 us
    all_to_all x1, waiting for transfers between devices, exchange(): lax.all_to_all(cut, ('depth', 'view'), split_axis=0, concat_axis=0, tiled...  3.13 us
    pallas_call x1, Pallas kernels, finish(): pl.pallas_call(functools.partial(finish_kernel, plan), in_specs=[SMEM, SM...  2.31 us
    pallas_call x1, Pallas kernels, message(): pl.pallas_call(functools.partial(assemble_kernel, plan, phase), in_specs=...  1.78 us
  transfers between devices with their start and end apart: 2, of which 1 were waited for; matrix products, arithmetic and copies ran while one was open for 1% of the time, Pallas kernels for 30%

profile of v1, /device:TPU:0, one launch (start us, length us, event | category | flops | bytes accessed | tf_op | source)
XLA Modules:
  0.0 56.2 jit_solution(10025056223404718072)
XLA Ops:
  0.0 0.7 %select_reduce_fusion = s32[8]{0:T(128)S(1)} fusion(s32[8]{0:T(128)} %bitcast.25), kind=kLoop, calls=%fused_computation.1 | loop fusion | flops 184 | bytes 64 | tf_op jit(solution)/shard_map/reduce_max | solution.py:414
  0.7 0.1 copy.5
  0.8 0.7 %pad.3.clone = s32[9]{0:T(128)S(1)} pad(s32[8]{0:T(128)} %bitcast.26, s32[]{:T(128)} %constant.14), padding=1_0 | pad | bytes 72 | tf_op jit(solution)/shard_map/concatenate | solution.py:415
  1.6 0.6 %broadcast_in_dim.32 = s32[4,8,9]{2,1,0:T(8,128)} broadcast(s32[8,9]{1,0:T(8,128)S(1)} %pad_add_fusion), dimensions={1,2} | broadcast | bytes 1440 | tf_op jit(solution)/shard_map/broadcast_in_dim | solution.py:418
  2.2 7.3 %all-to-all-start = ((s32[32,1,9]{2,1,0:T(1,128)}), s32[32,1,9]{2,1,0:T(1,128)S(1)}, u32[]{:S(2)}, u32[]{:S(2)}) async-start(s32[32,1,9]{2,1,0:T(1,128)} %bitcast.2), calls=%async_computation | async-start | bytes 32768 | tf_op jit(solution)/shard_map/all_to_all | solution.py:420
  9.5 0.7 %pad_add_fusion.1.me_ref.refs_1_ = s32[2]{0:T(128)} fusion(s32[1]{0:T(128)} %bitcast.5, s32[1]{0:T(128)} %bitcast.4), kind=kLoop, calls=%fused_computation.3 | loop fusion | flops 2 | bytes 16 | tf_op jit(solution)/shard_map/stack | solution.py:421
  10.1 7.9 %march_0.1.tiles_ref = f32[768,128]{1,0:T(8,128)} custom-call(f32[8,8,4,8,8,128]{5,4,3,2,1,0:T(8,128)} %bitcast.15), custom_call_target="tpu_custom_call" | custom-call | flops 31457280 | bytes 6291456 | tf_op jit(solution)/shard_map/march_0/pallas_call | solution.py:258
  18.1 0.0 all-to-all-done
  18.1 0.0 copy-start.1
  18.1 0.6 %copy-done.1 = s32[32,1,9]{2,1,0:T(1,128)} copy-done((s32[32,1,9]{2,1,0:T(1,128)}, s32[32,1,9]{2,1,0:T(1,128)S(1)}, u32[]{:S(2)}) %copy-start.1) | copy-done | bytes 1176
  18.7 1.8 %message_0.1 = f32[640,128]{1,0:T(8,128)} custom-call(s32[32,9]{1,0:T(8,128)} %bitcast.21, s32[2]{0:T(128)} %pad_add_fusion.1.me_ref.refs_1_, f32[768,128]{1,0:T(8,128)} %march_0.1.tiles_ref), custom_call_target="tpu_custom_call" | custom-call | tf_op jit(solution)/shard_map/message_0/pallas_call | solution.py:278
  20.5 5.8 %all-to-all-start.1 = ((f32[32,5,4,128]{3,2,1,0:T(4,128)}), f32[32,5,4,128]{3,2,1,0:T(4,128)S(1)}, u32[]{:S(2)}, u32[]{:S(2)}) async-start(f32[32,5,4,128]{3,2,1,0:T(4,128)} %bitcast.19), calls=%async_computation.1 | async-start | bytes 655360 | tf_op jit(solution)/shard_map/all_to_all | solution.py:403
  26.3 9.0 %march_1.1 = f32[640,128]{1,0:T(8,128)} custom-call(s32[32,9]{1,0:T(8,128)} %bitcast.22, s32[2]{0:T(128)} %pad_add_fusion.1.me_ref.refs_1_, f32[8,8,4,8,8,128]{5,4,3,2,1,0:T(8,128)} %bitcast.16), custom_call_target="tpu_custom_call" | custom-call | flops 31457280 | bytes 6291456 | tf_op jit(solution)/shard_map/march_1/pallas_call | solution.py:258
  35.3 3.1 %all-to-all-done.1 = f32[32,5,4,128]{3,2,1,0:T(4,128)S(1)} async-done(((f32[32,5,4,128]{3,2,1,0:T(4,128)}), f32[32,5,4,128]{3,2,1,0:T(4,128)S(1)}, u32[]{:S(2)}, u32[]{:S(2)}) %all-to-all-start.1) | async-done | bytes 327712 | tf_op jit(solution)/shard_map/all_to_all | solution.py:403
  38.4 0.0 copy-start
  38.4 15.4 %all_to_all.21 = f32[32,5,4,128]{3,2,1,0:T(4,128)} all-to-all(f32[32,5,4,128]{3,2,1,0:T(4,128)} %bitcast.17), channel_id=1, replica_groups=mesh['depth'=4,'view'=8] {'depth','view'}, dimensions={0} | all-to-all | bytes 655360 | tf_op jit(solution)/shard_map/all_to_all | solution.py:403
  53.9 0.0 copy-done
  53.9 2.3 %finish.1 = f32[4,16,512]{2,1,0:T(8,128)} custom-call(s32[32,9]{1,0:T(8,128)} %bitcast.23, s32[2]{0:T(128)} %pad_add_fusion.1.me_ref.refs_1_, f32[640,128]{1,0:T(8,128)} %bitcast.18, f32[640,128]{1,0:T(8,128)} %bitcast.20), custom_call_target="tpu_custom_call" | custom-call | tf_op jit(solution)/shard_map/finish/pallas_call | solution.py:389
  (1 shorter events, 0.0 us)
Async XLA Ops:
  2.2 15.9 %all-to-all-start = ((s32[32,1,9]{2,1,0:T(1,128)}), s32[32,1,9]{2,1,0:T(1,128)S(1)}, u32[]{:S(2)}, u32[]{:S(2)}) async-start(s32[32,1,9]{2,1,0:T(1,128)} %bitcast.2), calls=%async_computation | async-start | bytes 32768 | tf_op jit(solution)/shard_map/all_to_all | solution.py:420
  18.1 0.6 %copy-start.1 = (s32[32,1,9]{2,1,0:T(1,128)}, s32[32,1,9]{2,1,0:T(1,128)S(1)}, u32[]{:S(2)}) copy-start(s32[32,1,9]{2,1,0:T(1,128)S(1)} %all-to-all-done) | copy-start | bytes 3460
  20.5 18.0 %all-to-all-start.1 = ((f32[32,5,4,128]{3,2,1,0:T(4,128)}), f32[32,5,4,128]{3,2,1,0:T(4,128)S(1)}, u32[]{:S(2)}, u32[]{:S(2)}) async-start(f32[32,5,4,128]{3,2,1,0:T(4,128)} %bitcast.19), calls=%async_computation.1 | async-start | bytes 655360 | tf_op jit(solution)/shard_map/all_to_all | solution.py:403
  38.4 15.4 %copy-start = (f32[32,5,4,128]{3,2,1,0:T(4,128)}, f32[32,5,4,128]{3,2,1,0:T(4,128)S(1)}, u32[]{:S(2)}) copy-start(f32[32,5,4,128]{3,2,1,0:T(4,128)S(1)} %all-to-all-done.1) | copy-start | bytes 983044

commit v2 on v0

v2 whole, which is shorter than its diff:
```python
import functools

import jax
import jax.numpy as jnp
from jax import lax
from jax.experimental import pallas as pl
from jax.experimental.pallas import tpu as pltpu
from jax.sharding import PartitionSpec as P

STEPS = 48
DENSITY = 0.8
SHARPEN = 1.5
LANES = 128
EARLY = 2
MARCH_BYTES = 57 * 1024 * 1024
FINISH_BYTES = 16 * 1024 * 1024


class Plan:
    def __init__(self, depths, views, columns, edge, area):
        self.depths, self.views, self.columns = depths, views, columns
        self.pairs = area // LANES
        self.band = self.pairs // depths
        self.rows = 4 * self.band + 6
        self.peers = depths * views
        self.zts = edge // 8
        self.regs = self.pairs // 8
        self.run = min(self.regs, self.band)
        self.tops = [a for a in range(self.regs) if a % self.band == 0]
        self.bottoms = [a for a in range(self.regs) if (a + 1) % self.run == 0][-len(self.tops) :]
        self.blocks = 3 if len(self.tops) == 1 else 4

    def run_of(self, band):
        pair = band * self.band
        return pair // self.regs, pair % self.regs


def roll(x, shift, axis=1):
    return pltpu.roll(x, shift % x.shape[axis], axis)


def lane_of(shape):
    return lax.broadcasted_iota(jnp.int32, shape, 1)


def march_tile(plan, load):
    scale = DENSITY / (2 * STEPS)
    regs = plan.regs
    lane = lane_of((8, LANES))
    row = lax.broadcasted_iota(jnp.int32, (8, LANES), 0)
    low = lane < 64
    inside = (lane % 64 != 0).astype(jnp.float32)
    top, bottom = row == 0, row == 7
    third = 1.0 / 3.0

    def three(zt, part):
        planes = [[load(zt, 4 * part + r, a) for a in range(regs)] for r in range(4)]
        first = [(5.0 * third) * p + third * q for p, q in zip(planes[0], planes[1])]
        second = [p + q for p, q in zip(planes[1], planes[2])]
        last = [third * p + (5.0 * third) * q for p, q in zip(planes[2], planes[3])]
        return [first, second, last]

    def step(index, behind, here, ahead, carry):
        turned = [roll(x, 64) for x in here]
        after = jnp.where(bottom, here[-1], roll(turned[0], -1, 0))
        steps_y = [y - x for x, y in zip(turned, turned[1:] + [after])]
        before = jnp.where(top, turned[0] - here[0], roll(steps_y[-1], 1, 0))
        steps_y = [before] + steps_y
        out = []
        for a in range(regs):
            total, trans, lit, red, blue = carry[a]
            x = here[a]
            grad_y = jnp.where(low, steps_y[a], steps_y[a + 1])
            diff = (x - roll(x, 1)) * inside
            grad_x = diff + roll(diff, -1)
            grad_z = ahead[a] - behind[a]
            norm = grad_x * grad_x + grad_y * grad_y + (grad_z * grad_z + 4.0)
            slope = jnp.abs(grad_z) * lax.rsqrt(norm)
            total = total + jnp.tanh(x - 2.0)
            later = jnp.exp(total * -scale - scale * (index + 1))
            part = (trans - later) * (slope + 3.0 / 7.0)
            red = red + part * jnp.tanh(x * 0.375)
            blue = blue + part * jnp.tanh(x * 0.75 - 1.5)
            out.append((total, later, lit + part, red, blue))
        return out

    zero = jnp.zeros((8, LANES), jnp.float32)
    carry = [(zero, zero + 1.0, zero, zero, zero)] * regs
    samples = [x for zt in range(plan.zts) for part in range(2) for x in three(zt, part)]
    padded = samples[:1] + samples + samples[-1:]
    for index in range(STEPS):
        carry = step(index, *padded[index : index + 3], carry)
    value = [[], [], [], []]
    for _, trans, lit, red, blue in carry:
        value[0].append(0.35 * (lit + red))
        value[1].append(0.35 * (lit - red))
        value[2].append(0.35 * (lit + blue))
        value[3].append(1.0 - trans)
    return value


def store_tile(plan, value, tiles_ref, slot, first_slot):
    regs = plan.regs
    lane = lane_of((8, LANES))
    low = lane < 64
    rows = [(c // 2, c % 2 * regs + a, value[c][a]) for c in range(4) for a in range(regs)]
    spot = 0
    for a in plan.tops:
        for c in (0, 2):
            edge = jnp.where(low, value[c][a], roll(value[c + 1][a], 64))
            rows.append((2 + spot // 8, spot % 8, edge))
            spot += 1
    for a in plan.bottoms:
        for c in (0, 2):
            edge = jnp.where(low, roll(value[c][a], 64), value[c + 1][a])
            rows.append((2 + spot // 8, spot % 8, edge))
            spot += 1
    first = last = jnp.zeros((8, LANES), jnp.float32)
    for c in range(4):
        for a in range(regs):
            at = 4 * a + c
            first += roll(jnp.where(lane % 64 == 0, value[c][a], 0.0), at)
            last += roll(jnp.where(lane % 64 == 63, value[c][a], 0.0), 4 * regs + at - 63)
    rows.append((2 + spot // 8, spot % 8, jnp.where(first_slot, first, last)))
    for block, at, row in rows:
        tiles_ref[block, pl.ds(slot * 64 + at, 8, 8), :] = row


def assemble(plan, tiles_ref, route_ref, out_ref):
    depths, views, columns = plan.depths, plan.views, plan.columns
    regs, run, band_pairs = plan.regs, plan.run, plan.band
    mine = route_ref[0, columns]
    depth, view = mine // views, mine % views
    lane = lane_of((1, LANES))
    zero = jnp.zeros((1, LANES), jnp.float32)
    rim_at = 2 * len(plan.tops) + 2 * len(plan.bottoms)

    def rows_of(block, slot, sublane, at, count):
        return tiles_ref[block, pl.ds(slot * 64 + sublane * 8 + at, count), :]

    asked = []
    for v in range(views):
        found = jnp.int32(-1)
        for t in range(columns):
            found = jnp.where(route_ref[depth * views + v, t] == view, t, found)
        asked.append(found)

    def rim(slot, sublane):
        return rows_of(2 + rim_at // 8, slot, sublane, rim_at % 8, 1)

    def above_of(band):
        sublane, a = plan.run_of(band)
        return (sublane, a - 1) if a > 0 else (sublane - 1, regs - 1)

    def below_of(band):
        sublane, a = plan.run_of(band)
        sublane, a = sublane + (a + band_pairs) // regs, (a + band_pairs) % regs
        return sublane, a

    own, corner = {}, {}
    for slot in (0, columns - 1):
        for band in range(depths):
            sublane, a = plan.run_of(band)
            total = zero
            for i in range(band_pairs // run):
                total = total + roll(rim(slot, sublane + i), 8 * regs * i - 4 * a)
            own[slot, band] = total
            total = zero
            if band > 0:
                sublane, a = above_of(band)
                moved = roll(rim(slot, sublane), 4 * (regs - 1 - a))
                keep = (lane % (4 * regs) >= 4 * (regs - 1)) & (lane >= 64)
                total = total + jnp.where(keep, moved, 0.0)
            if band < depths - 1:
                sublane, a = below_of(band)
                moved = roll(rim(slot, sublane), -4 * a)
                keep = (lane % (4 * regs) < 4) & (lane < 64)
                total = total + jnp.where(keep, moved, 0.0)
            corner[slot, band] = total

    for v in range(views):
        slot = jnp.maximum(asked[v], 0)
        sides = []
        if v + 1 < views:
            sides.append((0, jnp.where(asked[v + 1] == 0, 1.0, 0.0)))
        if v > 0:
            sides.append((columns - 1, jnp.where(asked[v - 1] == columns - 1, 1.0, 0.0)))
        for band in range(depths):
            at = (band * views + v) * plan.rows
            first, a = plan.run_of(band)
            for c in range(4):
                for i in range(band_pairs // run):
                    start = at + c * band_pairs + i * run
                    out_ref[pl.ds(start, run), :] = rows_of(
                        c // 2, slot, first + i, c % 2 * regs + a, run
                    )
            at += 4 * band_pairs
            above = below = jnp.zeros((2, LANES), jnp.float32)
            if band > 0:
                sublane, a = above_of(band)
                place = 2 * len(plan.tops) + 2 * plan.bottoms.index(a)
                above = rows_of(2 + place // 8, slot, sublane, place % 8, 2)
            if band < depths - 1:
                sublane, a = below_of(band)
                place = 2 * plan.tops.index(a)
                below = rows_of(2 + place // 8, slot, sublane, place % 8, 2)
            out_ref[pl.ds(at, 2), :] = above
            out_ref[pl.ds(at + 2, 2), :] = below
            out_ref[pl.ds(at + 4, 1), :] = sum(own[s, band] * f for s, f in sides) + zero
            out_ref[pl.ds(at + 5, 1), :] = sum(corner[s, band] * f for s, f in sides) + zero


def march_planes(plan, planes, tiles_ref, slot, first_slot):
    flat = [ref.reshape(plan.zts * 64, LANES) for ref in planes]

    def load(zt, r, a):
        return flat[a][pl.ds(zt * 64 + r, 8, 8), :]

    store_tile(plan, march_tile(plan, load), tiles_ref, slot, first_slot)


def early_kernel(plan, *refs):
    planes, tiles_ref = refs[:-1], refs[-1]
    step = pl.program_id(0)
    march_planes(plan, planes, tiles_ref, step, step == 0)


def late_kernel(plan, early, *refs):
    route_ref, early_ref = refs[:2]
    planes, (out_ref, tiles_ref, sem) = refs[2:-3], refs[-3:]
    step = pl.program_id(0)
    copy = pltpu.make_async_copy(early_ref, tiles_ref.at[:, pl.ds(0, early * 64)], sem)

    @pl.when(step == 0)
    def _():
        copy.start()

    march_planes(plan, planes, tiles_ref, step + early, step + early == 0)

    @pl.when(step == plan.columns - early - 1)
    def _():
        copy.wait()
        assemble(plan, tiles_ref, route_ref, out_ref)


SMEM = pl.BlockSpec(memory_space=pltpu.SMEM)
PARAMS = pltpu.CompilerParams(vmem_limit_bytes=MARCH_BYTES)


def plane_specs(plan, start):
    shape = (1, plan.zts, 8, 1, 8, LANES)

    def spec(a):
        return pl.BlockSpec(shape, lambda i: (start + i, 0, 0, a, 0, 0))

    return [spec(a) for a in range(plan.regs)]


def cost(plan, count):
    samples = count * plan.pairs * LANES * STEPS
    return pl.CostEstimate(
        flops=40 * samples, bytes_accessed=6 * samples, transcendentals=5 * samples
    )


def march_early(plan, stored):
    tiles = (plan.blocks, EARLY * 64, LANES)
    return pl.pallas_call(
        functools.partial(early_kernel, plan),
        grid=(EARLY,),
        in_specs=plane_specs(plan, 0),
        out_specs=pl.BlockSpec(tiles, lambda i: (0, 0, 0)),
        out_shape=jax.ShapeDtypeStruct(tiles, jnp.float32),
        cost_estimate=cost(plan, EARLY),
        compiler_params=PARAMS,
        name="march_early",
    )(*[stored] * plan.regs)


def march_late(plan, stored, early, route):
    shape = (plan.peers * plan.rows, LANES)
    return pl.pallas_call(
        functools.partial(late_kernel, plan, EARLY),
        grid=(plan.columns - EARLY,),
        in_specs=[SMEM, pl.BlockSpec(memory_space=pl.ANY)] + plane_specs(plan, EARLY),
        out_specs=pl.BlockSpec(shape, lambda i: (0, 0)),
        out_shape=jax.ShapeDtypeStruct(shape, jnp.float32),
        scratch_shapes=[
            pltpu.VMEM((plan.blocks, plan.columns * 64, LANES), jnp.float32),
            pltpu.SemaphoreType.DMA(()),
        ],
        cost_estimate=cost(plan, plan.columns - EARLY),
        compiler_params=PARAMS,
        name="march_late",
    )(route, early, *[stored] * plan.regs)


def finish_kernel(plan, route_ref, source, out_ref, image):
    depths, views, band, columns = plan.depths, plan.views, plan.band, plan.columns
    regs = plan.regs
    lane = lane_of((1, LANES))
    low = lane < 64
    view = route_ref[0, columns] % views

    def over(front, alpha, back):
        return front if back is None else front + (1.0 - alpha) * back

    bodies, outers = [], []
    for t in range(columns):
        acc, rims = [None] * 4, [[None] * 2, [None] * 2]
        for d in reversed(range(depths)):
            holder = route_ref[d * views + view, t]
            shown = jnp.where(holder >= 0, 1.0, 0.0)
            at = (d * views + jnp.maximum(holder, 0)) * plan.rows
            front = [source[pl.ds(at + c * band, band), :] * shown for c in range(4)]
            acc = [over(f, front[3], b) for f, b in zip(front, acc)]
            for side in range(2):
                place = at + 4 * band + 2 * side
                front = [source[pl.ds(place + i, 1), :] * shown for i in range(2)]
                alpha = jnp.where(low, roll(front[1], 64), front[1])
                rims[side] = [over(f, alpha, b) for f, b in zip(front, rims[side])]
        bodies.append(acc)
        outers.append(rims)

    sides = None
    lane2 = lane_of((2, LANES))
    for d in reversed(range(depths)):
        front = None
        for h in range(views):
            piece = source[pl.ds((d * views + h) * plan.rows + 4 * band + 4, 2), :]
            front = piece if front is None else front + piece
        alpha = front
        for c in range(3):
            alpha = jnp.where(lane2 % 4 == c, roll(front, c - 3), alpha)
        sides = over(front, alpha, sides)

    count = 2 * band
    wide = lane_of((band, LANES))
    low_band = wide < 64
    number = lax.broadcasted_iota(jnp.int32, (band, LANES), 0)
    number = 8 * regs * (number // regs) + 4 * (number % regs)
    final = columns // 2 + 1
    spread = jnp.broadcast_to(sides[0:1], (band, LANES))
    for c in range(4):
        for u in range(columns // 2):
            x, y = bodies[2 * u][c], bodies[2 * u + 1][c]
            image[c, u + 1, pl.ds(8, band, 2), :] = jnp.where(low_band, x, roll(y, 64))
            image[c, u + 1, pl.ds(9, band, 2), :] = jnp.where(low_band, roll(x, 64), y)
            for side, at in ((0, 7), (1, 8 + count)):
                x, y = outers[2 * u][side][c // 2], outers[2 * u + 1][side][c // 2]
                if c % 2 == 0:
                    y = roll(y, 64)
                else:
                    x = roll(x, 64)
                image[c, u + 1, pl.ds(at, 1), :] = jnp.where(low, x, y)
        for base, tile, spot in ((0, final, 0), (4 * regs, 0, LANES - 1)):
            for odd in range(2):
                here = wide == base + 64 * odd + number + c
                column = jnp.sum(jnp.where(here, spread, 0.0), axis=1, keepdims=True)
                image[c, tile, pl.ds(8 + odd, band, 2), :] = jnp.where(wide == spot, column, 0.0)
            for at, place in ((7, 64 + base + 4 * (regs - 1) + c), (8 + count, base + c)):
                pixel = jnp.where(lane == place, sides[1:2], 0.0)
                pixel = jnp.sum(pixel, axis=1, keepdims=True)
                image[c, tile, pl.ds(at, 1), :] = jnp.where(lane == spot, pixel, 0.0)

    full = lane_of((count, LANES))
    for c in range(4):
        middle = [image[c, k, pl.ds(8, count), :] for k in range(final + 1)]
        smooth = [
            0.25 * image[c, k, pl.ds(7, count), :]
            + 0.5 * middle[k]
            + 0.25 * image[c, k, pl.ds(9, count), :]
            for k in range(final + 1)
        ]
        later = [roll(x, 1) for x in smooth]
        sooner = [roll(x, -1) for x in smooth]
        for k in range(1, final):
            left = jnp.where(full == 0, later[k - 1], later[k])
            right = jnp.where(full == LANES - 1, sooner[k + 1], sooner[k])
            blurred = 0.25 * left + 0.5 * smooth[k] + 0.25 * right
            out_ref[c, :, pl.ds((k - 1) * LANES, LANES)] = middle[k] + SHARPEN * (
                middle[k] - blurred
            )


def finish(plan, arrived, route):
    count = 2 * plan.band
    return pl.pallas_call(
        functools.partial(finish_kernel, plan),
        in_specs=[SMEM, pl.BlockSpec(memory_space=pltpu.VMEM)],
        out_specs=pl.BlockSpec(memory_space=pltpu.VMEM),
        out_shape=jax.ShapeDtypeStruct((4, count, plan.columns * 64), jnp.float32),
        scratch_shapes=[
            pltpu.VMEM((4, plan.columns // 2 + 2, count + 16, LANES), jnp.float32)
        ],
        compiler_params=pltpu.CompilerParams(vmem_limit_bytes=FINISH_BYTES),
        name="finish",
    )(route, arrived)


def exchange(plan, messages):
    cut = messages.reshape(plan.peers, plan.rows // 2, 2, LANES)
    moved = lax.all_to_all(cut, ("depth", "view"), split_axis=0, concat_axis=0, tiled=True)
    return moved.reshape(plan.peers * plan.rows, LANES)


def body(bricks, tile_holder):
    depths, views = lax.axis_size("depth"), lax.axis_size("view")
    columns, edge, area = bricks.shape[2:]
    plan = Plan(depths, views, columns, edge, area)
    number = jnp.arange(plan.peers, dtype=jnp.int32)[:, None, None]
    place = jnp.arange(columns + 1, dtype=jnp.int32)[None, None, :]
    request = jnp.pad(tile_holder, ((0, 0), (0, 0), (0, 1)))
    request = jnp.where(place == columns, number, request)
    route = lax.all_to_all(request, ("depth", "view"), split_axis=0, concat_axis=0, tiled=True)
    route = route.reshape(plan.peers, columns + 1)
    stored = bricks[0, 0].reshape(columns, plan.zts, 8, plan.pairs, LANES).transpose(0, 1, 3, 2, 4)
    stored = stored.reshape(columns, plan.zts, 8, plan.regs, 8, LANES)
    early = march_early(plan, stored)
    messages = march_late(plan, stored, early, route)
    return finish(plan, exchange(plan, messages), route)


def solution(mesh):
    in_specs = (P("depth", "view", None, None, None), P("depth", "view", None))
    out_specs = P(None, "depth", "view")
    return jax.shard_map(body, mesh=mesh, in_specs=in_specs, out_specs=out_specs, check_vma=False)
```

time: 308 us -> 50.6 us (0.16)
  waiting for transfers between devices: 199 us -> 2.73 us
  matrix products: 31.7 us -> 0 us
  local copies, waits for them, and re-layouts: 21.8 us -> 1.98 us
  Pallas kernels: 0 us -> 16 us
  loops' own time: 15.5 us -> 0 us
  blocking collectives: 11.7 us -> 21.6 us
  other arithmetic: 9.14 us -> 0.62 us
  starting transfers between devices: 15.5 us -> 7.3 us
    all_to_all x1, waiting for transfers between devices: 184 us -> 2.73 us  [body(): lax.all_to_all(request, ('depth', 'view'), split_axis=0, concat_axis=0, t...]
    dot_general x16 -> x0, matrix products: 31.7 us -> none  [the longest x8 16.7 us: march_brick(): samples = jnp.dot(table, brick, precision=lax.Precision.HIGHEST)]
    pallas_call x0 -> x3, Pallas kernels: none -> 16 us  [the longest x1 9.68 us: march_late(): pl.pallas_call(functools.partial(late_kernel, plan, EARLY), grid=(plan.co...]
    ppermute x6 -> x0, waiting for transfers between devices: 15.7 us -> none  [the longest x2 9.61 us: partner(): lax.ppermute(x, axis, [(i, i ^ 1 << stride) for i in range(lax.axis_size(...]
    another operation x1 -> x0, loops' own time: 15.5 us -> none  [body(): lax.map(lambda index_one: march_brick(arrived[index_one], table, prefix),...]
    ppermute x6 -> x0, starting transfers between devices: 10.4 us -> none  [the longest x2 4.68 us: padded_2(): before = lax.ppermute(last, axis, up)]
    all_to_all x1, blocking collectives: 11.7 us -> 21.6 us  [exchange(): lax.all_to_all(cut, ('depth', 'view'), split_axis=0, concat_axis=0, tiled...]
    gather x1 -> x0, local copies, waits for them, and re-layouts: 7.68 us -> none  [body(): outgoing = stored[slot_index]]
  transfers between devices with their start and end apart: 7 -> 1, of which waited for: 5 -> 1; matrix products, arithmetic and copies ran while one was open for 0% -> 0% of each run, Pallas kernels for 0% -> 9%
where the time goes in v2:
time: 50.6 us; the launch traced here: 50.2 us
  blocking collectives  21.6 us (43%)
  Pallas kernels  16 us (32%)
  starting transfers between devices  7.3 us (14%)
  waiting for transfers between devices  2.73 us (5%)
  local copies, waits for them, and re-layouts  1.98 us (4%)
  other arithmetic  0.62 us (1%)
    all_to_all x1, blocking collectives, exchange(): lax.all_to_all(cut, ('depth', 'view'), split_axis=0, concat_axis=0, tiled...  21.6 us
    pallas_call x1, Pallas kernels, march_late(): pl.pallas_call(functools.partial(late_kernel, plan, EARLY), grid=(plan.co...  9.68 us
    all_to_all x1, starting transfers between devices, body(): lax.all_to_all(request, ('depth', 'view'), split_axis=0, concat_axis=0, t...  7.3 us
    pallas_call x1, Pallas kernels, march_early(): pl.pallas_call(functools.partial(early_kernel, plan), grid=(EARLY,), in_s...  4.33 us
    all_to_all x1, waiting for transfers between devices, body(): lax.all_to_all(request, ('depth', 'view'), split_axis=0, concat_axis=0, t...  2.73 us
    pallas_call x1, Pallas kernels, finish(): pl.pallas_call(functools.partial(finish_kernel, plan), in_specs=[SMEM, pl...  1.99 us
    unnamed x4, local copies, waits for them, and re-layouts  1.32 us
  transfers between devices with their start and end apart: 1, of which 1 were waited for; matrix products, arithmetic and copies ran while one was open for 0% of the time, Pallas kernels for 9%

profile of v2, /device:TPU:0, one launch (start us, length us, event | category | flops | bytes accessed | tf_op | source)
XLA Modules:
  0.0 50.2 jit_solution(4817248961631562760)
XLA Ops:
  0.0 0.7 %pad_bitcast_fusion = s32[9]{0:T(128)S(1)} fusion(s32[1,1,8]{2,1,0:T(1,128)} %param.3), kind=kLoop, calls=%fused_computation.1 | loop fusion | bytes 68 | tf_op jit(solution)/shard_map/jit(_where)/broadcast_in_dim | solution.py:414
  0.7 0.6 %broadcast_select_fusion = s32[32,1,9]{2,1,0:T(1,128)} fusion(pred[9]{0:T(512)(128)(4,1)S(1)} %iota_compare_fusion, s32[9]{0:T(128)S(1)} %pad_bitcast_fusion), kind=kLoop, calls=%fused_computation | loop fusion | flops 288 | bytes 1197 | tf_op jit(solution)/shard_map/jit(_where)/select_n | solution.py:414
  1.3 7.3 %all-to-all-start = ((s32[32,1,9]{2,1,0:T(1,128)}), s32[32,1,9]{2,1,0:T(1,128)S(1)}, u32[]{:S(2)}, u32[]{:S(2)}) async-start(s32[32,1,9]{2,1,0:T(1,128)} %broadcast_select_fusion), calls=%async_computation | async-start | bytes 32768 | tf_op jit(solution)/shard_map/all_to_all | solution.py:415
  8.6 4.3 %march_early.1.refs_1_ = f32[3,128,128]{2,1,0:T(8,128)} custom-call(f32[8,8,8,4,8,128]{5,4,3,2,1,0:T(8,128)} %bitcast.13, f32[8,8,8,4,8,128]{5,4,3,2,1,0:T(8,128)} %bitcast.14, f32[8,8,8,4,8,128]{5,4,3,2,1,0:T(8,128)} %bitcast.15, f32[8,8,8,4,8,128]{5,4,3,2,1,0:T(8,128)} %bitcast.16), custom_call_target="tpu_custom_call" | custom-call | flops 15728640 | bytes 2359296 | tf_op jit(solution)/shard_map/march_early/pallas_call | solution.py:268
  12.9 2.7 %all-to-all-done = s32[32,1,9]{2,1,0:T(1,128)S(1)} async-done(((s32[32,1,9]{2,1,0:T(1,128)}), s32[32,1,9]{2,1,0:T(1,128)S(1)}, u32[]{:S(2)}, u32[]{:S(2)}) %all-to-all-start) | async-done | bytes 1184 | tf_op jit(solution)/shard_map/all_to_all | solution.py:415
  15.7 0.0 copy-start
  15.7 0.6 %copy-done = s32[32,1,9]{2,1,0:T(1,128)} copy-done((s32[32,1,9]{2,1,0:T(1,128)}, s32[32,1,9]{2,1,0:T(1,128)S(1)}, u32[]{:S(2)}) %copy-start) | copy-done | bytes 1176
  16.3 9.7 %march_late.1 = f32[1216,128]{1,0:T(8,128)} custom-call(s32[32,9]{1,0:T(8,128)} %bitcast.11, f32[3,128,128]{2,1,0:T(8,128)} %march_early.1.refs_1_, f32[8,8,8,4,8,128]{5,4,3,2,1,0:T(8,128)} %bitcast.17, f32[8,8,8,4,8,128]{5,4,3,2,1,0:T(8,128)} %bitcast.18, f32[8,8,8,4,8,128]{5,4,3,2,1,0:T(8,128)} %bitcast.19, f32[8,8,8,4,8,128]{5,4,3,2,1,0:T(8,128)} %bitcast.20), custom_call_target="tpu_custom_call" | custom-call | flops 47185920 | bytes 7077888 | tf_op jit(solution)/shard_map/march_late/pallas_call | solution.py:282
  26.0 21.6 %all_to_all.10 = f32[32,19,2,128]{3,2,1,0:T(2,128)S(1)} all-to-all(f32[32,19,2,128]{3,2,1,0:T(2,128)} %bitcast.21), channel_id=1, replica_groups=mesh['depth'=4,'view'=8] {'depth','view'}, dimensions={0} | all-to-all | bytes 1245184 | tf_op jit(solution)/shard_map/all_to_all | solution.py:403
  47.5 0.0 copy-start.1
  47.5 0.7 %copy-done.1 = s32[32,1,9]{2,1,0:T(1,128)S(1)} copy-done((s32[32,1,9]{2,1,0:T(1,128)S(1)}, s32[32,1,9]{2,1,0:T(1,128)}, u32[]{:S(2)}) %copy-start.1) | copy-done | bytes 1176
  48.3 2.0 %finish.1 = f32[4,16,512]{2,1,0:T(8,128)} custom-call(s32[32,9]{1,0:T(8,128)S(1)} %bitcast.12, f32[1216,128]{1,0:T(8,128)S(1)} %bitcast.10), custom_call_target="tpu_custom_call" | custom-call | tf_op jit(solution)/shard_map/finish/pallas_call | solution.py:388
  (1 shorter events, 0.0 us)
Async XLA Ops:
  1.3 14.4 %all-to-all-start = ((s32[32,1,9]{2,1,0:T(1,128)}), s32[32,1,9]{2,1,0:T(1,128)S(1)}, u32[]{:S(2)}, u32[]{:S(2)}) async-start(s32[32,1,9]{2,1,0:T(1,128)} %broadcast_select_fusion), calls=%async_computation | async-start | bytes 32768 | tf_op jit(solution)/shard_map/all_to_all | solution.py:415
  15.7 0.6 %copy-start = (s32[32,1,9]{2,1,0:T(1,128)}, s32[32,1,9]{2,1,0:T(1,128)S(1)}, u32[]{:S(2)}) copy-start(s32[32,1,9]{2,1,0:T(1,128)S(1)} %all-to-all-done) | copy-start | bytes 3460
  47.5 0.7 %copy-start.1 = (s32[32,1,9]{2,1,0:T(1,128)S(1)}, s32[32,1,9]{2,1,0:T(1,128)}, u32[]{:S(2)}) copy-start(s32[32,1,9]{2,1,0:T(1,128)} %copy-done) | copy-start | bytes 3460

commit v3 on v2

--- a/solution.py
+++ b/solution.py
@@ -11,9 +11,8 @@
 DENSITY = 0.8
 SHARPEN = 1.5
 LANES = 128
-EARLY = 2
-MARCH_BYTES = 57 * 1024 * 1024
-FINISH_BYTES = 16 * 1024 * 1024
+PEERS = ("depth", "view")
+VMEM_BYTES = 16 * 1024 * 1024
 
 
 class Plan:
@@ -29,6 +28,9 @@
         self.tops = [a for a in range(self.regs) if a % self.band == 0]
         self.bottoms = [a for a in range(self.regs) if (a + 1) % self.run == 0][-len(self.tops) :]
         self.blocks = 3 if len(self.tops) == 1 else 4
+
+    def peer(self, depth, view):
+        return depth * self.views + view
 
     def run_of(self, band):
         pair = band * self.band
@@ -76,11 +78,12 @@
             grad_z = ahead[a] - behind[a]
             norm = grad_x * grad_x + grad_y * grad_y + (grad_z * grad_z + 4.0)
             slope = jnp.abs(grad_z) * lax.rsqrt(norm)
-            total = total + jnp.tanh(x - 2.0)
+            above = x - 2.0
+            total = total + jnp.tanh(above)
             later = jnp.exp(total * -scale - scale * (index + 1))
             part = (trans - later) * (slope + 3.0 / 7.0)
             red = red + part * jnp.tanh(x * 0.375)
-            blue = blue + part * jnp.tanh(x * 0.75 - 1.5)
+            blue = blue + part * jnp.tanh(above * 0.75)
             out.append((total, later, lit + part, red, blue))
         return out
 
@@ -99,7 +102,7 @@
     return value
 
 
-def store_tile(plan, value, tiles_ref, slot, first_slot):
+def store_tile(plan, value, tiles_ref, slot):
     regs = plan.regs
     lane = lane_of((8, LANES))
     low = lane < 64
@@ -115,22 +118,25 @@
             edge = jnp.where(low, roll(value[c][a], 64), value[c + 1][a])
             rows.append((2 + spot // 8, spot % 8, edge))
             spot += 1
-    first = last = jnp.zeros((8, LANES), jnp.float32)
-    for c in range(4):
-        for a in range(regs):
-            at = 4 * a + c
-            first += roll(jnp.where(lane % 64 == 0, value[c][a], 0.0), at)
-            last += roll(jnp.where(lane % 64 == 63, value[c][a], 0.0), 4 * regs + at - 63)
-    rows.append((2 + spot // 8, spot % 8, jnp.where(first_slot, first, last)))
     for block, at, row in rows:
-        tiles_ref[block, pl.ds(slot * 64 + at, 8, 8), :] = row
-
-
-def assemble(plan, tiles_ref, route_ref, out_ref):
+        tiles_ref[block, pl.ds(at, 8, 8), :] = row
+    for number, column, base in ((0, 0, 0), (plan.columns - 1, 63, 4 * regs)):
+
+        @pl.when(slot == number)
+        def _():
+            rim = jnp.zeros((8, LANES), jnp.float32)
+            for c in range(4):
+                for a in range(regs):
+                    pixels = jnp.where(lane % 64 == column, value[c][a], 0.0)
+                    rim += roll(pixels, base + 4 * a + c - column)
+            tiles_ref[2 + spot // 8, pl.ds(spot % 8, 8, 8), :] = rim
+
+
+def message_kernel(plan, view_ref, *refs):
     depths, views, columns = plan.depths, plan.views, plan.columns
     regs, run, band_pairs = plan.regs, plan.run, plan.band
-    mine = route_ref[0, columns]
-    depth, view = mine // views, mine % views
+    route_refs, (tiles_ref, out_ref, asked_ref) = refs[:-3], refs[-3:]
+    view = view_ref[0]
     lane = lane_of((1, LANES))
     zero = jnp.zeros((1, LANES), jnp.float32)
     rim_at = 2 * len(plan.tops) + 2 * len(plan.bottoms)
@@ -138,12 +144,13 @@
     def rows_of(block, slot, sublane, at, count):
         return tiles_ref[block, pl.ds(slot * 64 + sublane * 8 + at, count), :]
 
-    asked = []
-    for v in range(views):
-        found = jnp.int32(-1)
-        for t in range(columns):
-            found = jnp.where(route_ref[depth * views + v, t] == view, t, found)
-        asked.append(found)
+    for i, route_ref in enumerate(route_refs):
+        for r in range(2):
+            found = jnp.int32(-1)
+            for t in range(columns):
+                found = jnp.where(route_ref[r, t] == view, t, found)
+            asked_ref[view ^ (2 * i + r)] = found
+    asked = [asked_ref[v] for v in range(views)]
 
     def rim(slot, sublane):
         return rows_of(2 + rim_at // 8, slot, sublane, rim_at % 8, 1)
@@ -186,7 +193,7 @@
         if v > 0:
             sides.append((columns - 1, jnp.where(asked[v - 1] == columns - 1, 1.0, 0.0)))
         for band in range(depths):
-            at = (band * views + v) * plan.rows
+            at = plan.peer(band, v) * plan.rows
             first, a = plan.run_of(band)
             for c in range(4):
                 for i in range(band_pairs // run):
@@ -207,132 +214,130 @@
             out_ref[pl.ds(at, 2), :] = above
             out_ref[pl.ds(at + 2, 2), :] = below
             out_ref[pl.ds(at + 4, 1), :] = sum(own[s, band] * f for s, f in sides) + zero
-            out_ref[pl.ds(at + 5, 1), :] = sum(corner[s, band] * f for s, f in sides) + zero
-
-
-def march_planes(plan, planes, tiles_ref, slot, first_slot):
-    flat = [ref.reshape(plan.zts * 64, LANES) for ref in planes]
-
-    def load(zt, r, a):
-        return flat[a][pl.ds(zt * 64 + r, 8, 8), :]
-
-    store_tile(plan, march_tile(plan, load), tiles_ref, slot, first_slot)
-
-
-def early_kernel(plan, *refs):
-    planes, tiles_ref = refs[:-1], refs[-1]
+            mark = jnp.where(lane == LANES - 1, asked[v].astype(jnp.float32), 0.0)
+            out_ref[pl.ds(at + 5, 1), :] = sum(corner[s, band] * f for s, f in sides) + mark
+
+
+def march_kernel(plan, x_ref, pair_ref, out_ref, held, sems):
     step = pl.program_id(0)
-    march_planes(plan, planes, tiles_ref, step, step == 0)
-
-
-def late_kernel(plan, early, *refs):
-    route_ref, early_ref = refs[:2]
-    planes, (out_ref, tiles_ref, sem) = refs[2:-3], refs[-3:]
-    step = pl.program_id(0)
-    copy = pltpu.make_async_copy(early_ref, tiles_ref.at[:, pl.ds(0, early * 64)], sem)
+
+    def copies(slot):
+        parity = slot % 2
+        return [
+            pltpu.make_async_copy(
+                x_ref.at[slot, :, :, a], held.at[parity, :, a], sems.at[parity, a]
+            )
+            for a in range(plan.regs)
+        ]
 
     @pl.when(step == 0)
     def _():
-        copy.start()
-
-    march_planes(plan, planes, tiles_ref, step + early, step + early == 0)
-
-    @pl.when(step == plan.columns - early - 1)
+        for copy in copies(step):
+            copy.start()
+
+    @pl.when(step + 1 < plan.columns)
     def _():
+        for copy in copies(step + 1):
+            copy.start()
+
+    for copy in copies(step):
         copy.wait()
-        assemble(plan, tiles_ref, route_ref, out_ref)
+
+    size = plan.zts * plan.regs * 64
+    flat = held.reshape(2 * size, LANES)
+    origin = (step % 2) * size
+
+    def load(zt, r, a):
+        return flat[pl.ds(origin + (zt * plan.regs + a) * 64 + r, 8, 8), :]
+
+    store_tile(plan, march_tile(plan, load), out_ref, step)
 
 
 SMEM = pl.BlockSpec(memory_space=pltpu.SMEM)
-PARAMS = pltpu.CompilerParams(vmem_limit_bytes=MARCH_BYTES)
-
-
-def plane_specs(plan, start):
-    shape = (1, plan.zts, 8, 1, 8, LANES)
-
-    def spec(a):
-        return pl.BlockSpec(shape, lambda i: (start + i, 0, 0, a, 0, 0))
-
-    return [spec(a) for a in range(plan.regs)]
-
-
-def cost(plan, count):
-    samples = count * plan.pairs * LANES * STEPS
-    return pl.CostEstimate(
-        flops=40 * samples, bytes_accessed=6 * samples, transcendentals=5 * samples
-    )
-
-
-def march_early(plan, stored):
-    tiles = (plan.blocks, EARLY * 64, LANES)
+VMEM = pl.BlockSpec(memory_space=pltpu.VMEM)
+PARAMS = pltpu.CompilerParams(vmem_limit_bytes=VMEM_BYTES)
+
+
+def march(plan, stored, pair):
+    samples = plan.columns * plan.pairs * LANES * STEPS
     return pl.pallas_call(
-        functools.partial(early_kernel, plan),
-        grid=(EARLY,),
-        in_specs=plane_specs(plan, 0),
-        out_specs=pl.BlockSpec(tiles, lambda i: (0, 0, 0)),
-        out_shape=jax.ShapeDtypeStruct(tiles, jnp.float32),
-        cost_estimate=cost(plan, EARLY),
+        functools.partial(march_kernel, plan),
+        grid=(plan.columns,),
+        in_specs=[pl.BlockSpec(memory_space=pltpu.HBM), pl.BlockSpec(memory_space=pl.ANY)],
+        out_specs=pl.BlockSpec((plan.blocks, 64, LANES), lambda i: (0, i, 0)),
+        out_shape=jax.ShapeDtypeStruct((plan.blocks, plan.columns * 64, LANES), jnp.float32),
+        scratch_shapes=[
+            pltpu.VMEM((2, plan.zts, plan.regs, 8, 8, LANES), jnp.float32),
+            pltpu.SemaphoreType.DMA((2, plan.regs)),
+        ],
+        cost_estimate=pl.CostEstimate(
+            flops=40 * samples, bytes_accessed=6 * samples, transcendentals=5 * samples
+        ),
+        compiler_params=pltpu.CompilerParams(vmem_limit_bytes=50*1024*1024),
+        name="march",
+    )(stored, pair)
+
+
+def message(plan, view, routes, tiles):
+    return pl.pallas_call(
+        functools.partial(message_kernel, plan),
+        in_specs=[SMEM] + [SMEM] * len(routes) + [VMEM],
+        out_specs=VMEM,
+        out_shape=jax.ShapeDtypeStruct((plan.peers * plan.rows, LANES), jnp.float32),
+        scratch_shapes=[pltpu.SMEM((plan.views,), jnp.int32)],
         compiler_params=PARAMS,
-        name="march_early",
-    )(*[stored] * plan.regs)
-
-
-def march_late(plan, stored, early, route):
-    shape = (plan.peers * plan.rows, LANES)
-    return pl.pallas_call(
-        functools.partial(late_kernel, plan, EARLY),
-        grid=(plan.columns - EARLY,),
-        in_specs=[SMEM, pl.BlockSpec(memory_space=pl.ANY)] + plane_specs(plan, EARLY),
-        out_specs=pl.BlockSpec(shape, lambda i: (0, 0)),
-        out_shape=jax.ShapeDtypeStruct(shape, jnp.float32),
-        scratch_shapes=[
-            pltpu.VMEM((plan.blocks, plan.columns * 64, LANES), jnp.float32),
-            pltpu.SemaphoreType.DMA(()),
-        ],
-        cost_estimate=cost(plan, plan.columns - EARLY),
-        compiler_params=PARAMS,
-        name="march_late",
-    )(route, early, *[stored] * plan.regs)
-
-
-def finish_kernel(plan, route_ref, source, out_ref, image):
+        name="message",
+    )(view, *routes, tiles)
+
+
+def finish_kernel(plan, source, out_ref, image, marks):
     depths, views, band, columns = plan.depths, plan.views, plan.band, plan.columns
     regs = plan.regs
     lane = lane_of((1, LANES))
     low = lane < 64
-    view = route_ref[0, columns] % views
 
     def over(front, alpha, back):
         return front if back is None else front + (1.0 - alpha) * back
-
-    bodies, outers = [], []
-    for t in range(columns):
-        acc, rims = [None] * 4, [[None] * 2, [None] * 2]
-        for d in reversed(range(depths)):
-            holder = route_ref[d * views + view, t]
-            shown = jnp.where(holder >= 0, 1.0, 0.0)
-            at = (d * views + jnp.maximum(holder, 0)) * plan.rows
-            front = [source[pl.ds(at + c * band, band), :] * shown for c in range(4)]
-            acc = [over(f, front[3], b) for f, b in zip(front, acc)]
-            for side in range(2):
-                place = at + 4 * band + 2 * side
-                front = [source[pl.ds(place + i, 1), :] * shown for i in range(2)]
-                alpha = jnp.where(low, roll(front[1], 64), front[1])
-                rims[side] = [over(f, alpha, b) for f, b in zip(front, rims[side])]
-        bodies.append(acc)
-        outers.append(rims)
 
     sides = None
     lane2 = lane_of((2, LANES))
     for d in reversed(range(depths)):
         front = None
         for h in range(views):
-            piece = source[pl.ds((d * views + h) * plan.rows + 4 * band + 4, 2), :]
+            n = plan.peer(d, h)
+            piece = source[pl.ds(n * plan.rows + 4 * band + 4, 2), :]
             front = piece if front is None else front + piece
+            mark = jnp.where(lane == LANES - 1, piece[1:2], 0.0)
+            mark = jnp.sum(mark, axis=1, keepdims=True)
+            marks[n] = jnp.broadcast_to(mark, (8, LANES))
         alpha = front
         for c in range(3):
             alpha = jnp.where(lane2 % 4 == c, roll(front, c - 3), alpha)
         sides = over(front, alpha, sides)
+
+    bodies, outers = [], []
+    low4 = lane_of((4, LANES)) < 64
+    even4 = lax.broadcasted_iota(jnp.int32, (4, LANES), 0) % 2 == 0
+    for t in range(columns):
+        acc, rims = [None] * 4, None
+        for d in reversed(range(depths)):
+            front = [jnp.zeros((band, LANES), jnp.float32)] * 4
+            rim = jnp.zeros((4, LANES), jnp.float32)
+            for h in range(views):
+                n = plan.peer(d, h)
+                at = n * plan.rows
+                chosen = marks[n] == t
+                front = [
+                    jnp.where(chosen[:band], source[pl.ds(at + c * band, band), :], x)
+                    for c, x in enumerate(front)
+                ]
+                rim = jnp.where(chosen[:4], source[pl.ds(at + 4 * band, 4), :], rim)
+            acc = [over(f, front[3], b) for f, b in zip(front, acc)]
+            alpha = jnp.where(low4, roll(rim, 64), rim)
+            alpha = jnp.where(even4, roll(alpha, -1, 0), alpha)
+            rims = over(rim, alpha, rims)
+        bodies.append(acc)
+        outers.append([[rims[2 * side + i : 2 * side + i + 1] for i in range(2)] for side in range(2)])
 
     count = 2 * band
     wide = lane_of((band, LANES))
@@ -383,42 +388,45 @@
             )
 
 
-def finish(plan, arrived, route):
+def finish(plan, arrived):
     count = 2 * plan.band
     return pl.pallas_call(
         functools.partial(finish_kernel, plan),
-        in_specs=[SMEM, pl.BlockSpec(memory_space=pltpu.VMEM)],
-        out_specs=pl.BlockSpec(memory_space=pltpu.VMEM),
+        in_specs=[VMEM],
+        out_specs=VMEM,
         out_shape=jax.ShapeDtypeStruct((4, count, plan.columns * 64), jnp.float32),
         scratch_shapes=[
-            pltpu.VMEM((4, plan.columns // 2 + 2, count + 16, LANES), jnp.float32)
+            pltpu.VMEM((4, plan.columns // 2 + 2, count + 16, LANES), jnp.float32),
+            pltpu.VMEM((plan.peers, 8, LANES), jnp.float32),
         ],
-        compiler_params=pltpu.CompilerParams(vmem_limit_bytes=FINISH_BYTES),
+        compiler_params=PARAMS,
         name="finish",
-    )(route, arrived)
+    )(arrived)
 
 
 def exchange(plan, messages):
     cut = messages.reshape(plan.peers, plan.rows // 2, 2, LANES)
-    moved = lax.all_to_all(cut, ("depth", "view"), split_axis=0, concat_axis=0, tiled=True)
+    moved = lax.all_to_all(cut, PEERS, split_axis=0, concat_axis=0, tiled=True)
     return moved.reshape(plan.peers * plan.rows, LANES)
+
+
+def swapped(x, distance):
+    pairs = [(i, i ^ distance) for i in range(lax.axis_size("view"))]
+    return lax.ppermute(x, "view", pairs)
 
 
 def body(bricks, tile_holder):
     depths, views = lax.axis_size("depth"), lax.axis_size("view")
     columns, edge, area = bricks.shape[2:]
     plan = Plan(depths, views, columns, edge, area)
-    number = jnp.arange(plan.peers, dtype=jnp.int32)[:, None, None]
-    place = jnp.arange(columns + 1, dtype=jnp.int32)[None, None, :]
-    request = jnp.pad(tile_holder, ((0, 0), (0, 0), (0, 1)))
-    request = jnp.where(place == columns, number, request)
-    route = lax.all_to_all(request, ("depth", "view"), split_axis=0, concat_axis=0, tiled=True)
-    route = route.reshape(plan.peers, columns + 1)
+    view = lax.axis_index("view").astype(jnp.int32).reshape(1)
+    own = tile_holder.reshape(1, columns)
+    pair = jnp.concatenate([own, swapped(own, 1)], axis=0)
+    routes = [pair] + [swapped(pair, k) for k in range(2, views, 2)]
     stored = bricks[0, 0].reshape(columns, plan.zts, 8, plan.pairs, LANES).transpose(0, 1, 3, 2, 4)
     stored = stored.reshape(columns, plan.zts, 8, plan.regs, 8, LANES)
-    early = march_early(plan, stored)
-    messages = march_late(plan, stored, early, route)
-    return finish(plan, exchange(plan, messages), route)
+    messages = message(plan, view, routes, march(plan, stored, pair))
+    return finish(plan, exchange(plan, messages))
 
 
 def solution(mesh):

time: 50.6 us -> 45.6 us (0.901)
  blocking collectives: 21.6 us -> 24.3 us
  Pallas kernels: 16 us -> 13.5 us
  local copies, waits for them, and re-layouts: 1.98 us -> 0 us
  waiting for transfers between devices: 2.73 us -> 0.96 us
  starting transfers between devices: 7.3 us -> 5.98 us
    all_to_all x1 -> x0, starting transfers between devices: 7.3 us -> none  [body(): lax.all_to_all(request, ('depth', 'view'), split_axis=0, concat_axis=0, t...]
    ppermute x0 -> x4, starting transfers between devices: none -> 5.98 us  [swapped(): return lax.ppermute(x, 'view', pairs)]
    all_to_all x1 -> x0, waiting for transfers between devices: 2.73 us -> none  [body(): lax.all_to_all(request, ('depth', 'view'), split_axis=0, concat_axis=0, t...]
    all_to_all x1, blocking collectives: 21.6 us -> 24.3 us  [exchange(): moved = lax.all_to_all(cut, PEERS, split_axis=0, concat_axis=0, tiled=True)]
    pallas_call x3, Pallas kernels: 16 us -> 13.5 us  [the longest x1 11.3 us: march(): pl.pallas_call(functools.partial(march_kernel, plan), grid=(plan.columns,...]
    unnamed x4 -> x0, local copies, waits for them, and re-layouts: 1.32 us -> none
    ppermute x0 -> x4, waiting for transfers between devices: none -> 0.96 us  [swapped(): return lax.ppermute(x, 'view', pairs)]
    concatenate x0 -> x1, other arithmetic: none -> 0.66 us  [body(): pair = jnp.concatenate([own, swapped(own, 1)], axis=0)]
  transfers between devices with their start and end apart: 1 -> 4, of which waited for: 1 -> 1; matrix products, arithmetic and copies ran while one was open for 0% -> 0% of each run, Pallas kernels for 9% -> 25%
where the time goes in v3:
time: 45.6 us; the launch traced here: 45.4 us
  blocking collectives  24.3 us (53%)
  Pallas kernels  13.5 us (30%)
  starting transfers between devices  5.98 us (13%)
  waiting for transfers between devices  0.96 us (2%)
  other arithmetic  0.66 us (1%)
    all_to_all x1, blocking collectives, exchange(): moved = lax.all_to_all(cut, PEERS, split_axis=0, concat_axis=0, tiled=True)  24.3 us
    pallas_call x1, Pallas kernels, march(): pl.pallas_call(functools.partial(march_kernel, plan), grid=(plan.columns,...  11.3 us
    ppermute x4, starting transfers between devices, swapped(): return lax.ppermute(x, 'view', pairs)  5.98 us
    pallas_call x1, Pallas kernels, finish(): pl.pallas_call(functools.partial(finish_kernel, plan), in_specs=[VMEM], o...  1.41 us
    ppermute x4, waiting for transfers between devices, swapped(): return lax.ppermute(x, 'view', pairs)  0.96 us
  transfers between devices with their start and end apart: 4, of which 1 were waited for; matrix products, arithmetic and copies ran while one was open for 0% of the time, Pallas kernels for 25%

profile of v3, /device:TPU:0, one launch (start us, length us, event | category | flops | bytes accessed | tf_op | source)
XLA Modules:
  0.0 45.4 jit_solution(9990242911434130782)
XLA Ops:
  0.0 0.5 collective-permute-start
  0.5 1.0 %collective-permute-done = s32[1,8]{1,0:T(1,128)S(1)} collective-permute-done((s32[1,8]{1,0:T(1,128)}, s32[1,8]{1,0:T(1,128)S(1)}, u32[]{:S(2)}, u32[]{:S(2)}) %collective-permute-start) | collective-permute-done | bytes 64 | tf_op jit(solution)/shard_map/ppermute | solution.py:415
  1.4 0.7 %pad_add_fusion.pair_ref.refs_0_ = s32[2,8]{1,0:T(2,128)S(1)} fusion(s32[1,8]{1,0:T(1,128)S(1)} %collective-permute-done, s32[1,8]{1,0:T(1,128)} %bitcast.12), kind=kLoop, calls=%fused_computation | loop fusion | flops 16 | bytes 128 | tf_op jit(solution)/shard_map/concatenate | solution.py:424
  2.1 4.9 %collective-permute-start.3 = (s32[2,8]{1,0:T(2,128)S(1)}, s32[2,8]{1,0:T(2,128)S(1)}, u32[]{:S(2)}, u32[]{:S(2)}) collective-permute-start(s32[2,8]{1,0:T(2,128)S(1)} %pad_add_fusion.pair_ref.refs_0_), channel_id=1, source_target_pairs={{0,6},{1,7},{2,4},{3,5},{4,2},{5,3},{6,0},{7,1},{8,14},{9,15},{10,... | collective-permute-start | bytes 200 | tf_op jit(solution)/shard_map/ppermute | solution.py:415
  7.0 0.0 collective-permute-start.2
  7.0 0.6 %collective-permute-start.1 = (s32[2,8]{1,0:T(2,128)S(1)}, s32[2,8]{1,0:T(2,128)S(1)}, u32[]{:S(2)}, u32[]{:S(2)}) collective-permute-start(s32[2,8]{1,0:T(2,128)S(1)} %pad_add_fusion.pair_ref.refs_0_), channel_id=1, source_target_pairs={{0,2},{1,3},{2,0},{3,1},{4,6},{5,7},{6,4},{7,5},{8,10},{9,11},{10,... | collective-permute-start | bytes 200 | tf_op jit(solution)/shard_map/ppermute | solution.py:415
  7.6 11.3 %march.1.refs_4_ = f32[3,512,128]{2,1,0:T(8,128)S(1)} custom-call(f32[8,8,8,4,8,128]{5,4,3,2,1,0:T(8,128)} %bitcast.13, s32[2,8]{1,0:T(2,128)S(1)} %pad_add_fusion.pair_ref.refs_0_), custom_call_target="tpu_custom_call" | custom-call | flops 62914560 | bytes 9437184 | tf_op jit(solution)/shard_map/march/pallas_call | solution.py:263
  18.9 0.0 collective-permute-done.3.refs_3_
  18.9 0.0 collective-permute-done.2.refs_2_
  18.9 0.0 collective-permute-done.1.refs_1_
  18.9 0.8 %message.1 = f32[1216,128]{1,0:T(8,128)S(1)} custom-call(s32[1]{0:T(128)} %bitcast.view_ref, s32[2,8]{1,0:T(2,128)S(1)} %pad_add_fusion.pair_ref.refs_0_, s32[2,8]{1,0:T(2,128)S(1)} %collective-permute-done.1.refs_1_, s32[2,8]{1,0:T(2,128)S(1)} %collective-permute-done.2.refs_2_, s32[2,8]{1,0:T(2,128)S(1)} %collective-permute-done.3.refs_3_, ...), custom_call_target="tpu_custom_call" | custom-call | tf_op jit(solution)/shard_map/message/pallas_call | solution.py:282
  19.7 24.3 %all_to_all.5 = f32[32,19,2,128]{3,2,1,0:T(2,128)S(1)} all-to-all(f32[32,19,2,128]{3,2,1,0:T(2,128)S(1)} %bitcast.9), channel_id=1, replica_groups=mesh['depth'=4,'view'=8] {'depth','view'}, dimensions={0} | all-to-all | bytes 1245184 | tf_op jit(solution)/shard_map/all_to_all | solution.py:409
  44.0 1.4 %finish.1 = f32[4,16,512]{2,1,0:T(8,128)} custom-call(f32[1216,128]{1,0:T(8,128)S(1)} %bitcast.10), custom_call_target="tpu_custom_call" | custom-call | tf_op jit(solution)/shard_map/finish/pallas_call | solution.py:393
Async XLA Ops:
  0.0 1.4 %collective-permute-start = (s32[1,8]{1,0:T(1,128)}, s32[1,8]{1,0:T(1,128)S(1)}, u32[]{:S(2)}, u32[]{:S(2)}) collective-permute-start(s32[1,8]{1,0:T(1,128)} %bitcast.11), channel_id=1, source_target_pairs={{0,1},{1,0},{2,3},{3,2},{4,5},{5,4},{6,7},{7,6},{8,9},{9,8},{10,11... | collective-permute-start | bytes 104 | tf_op jit(solution)/shard_map/ppermute | solution.py:415
  2.1 16.8 %collective-permute-start.3 = (s32[2,8]{1,0:T(2,128)S(1)}, s32[2,8]{1,0:T(2,128)S(1)}, u32[]{:S(2)}, u32[]{:S(2)}) collective-permute-start(s32[2,8]{1,0:T(2,128)S(1)} %pad_add_fusion.pair_ref.refs_0_), channel_id=1, source_target_pairs={{0,6},{1,7},{2,4},{3,5},{4,2},{5,3},{6,0},{7,1},{8,14},{9,15},{10,... | collective-permute-start | bytes 200 | tf_op jit(solution)/shard_map/ppermute | solution.py:415
  7.0 11.9 %collective-permute-start.2 = (s32[2,8]{1,0:T(2,128)S(1)}, s32[2,8]{1,0:T(2,128)S(1)}, u32[]{:S(2)}, u32[]{:S(2)}) collective-permute-start(s32[2,8]{1,0:T(2,128)S(1)} %pad_add_fusion.pair_ref.refs_0_), channel_id=1, source_target_pairs={{0,4},{1,5},{2,6},{3,7},{4,0},{5,1},{6,2},{7,3},{8,12},{9,13},{10,... | collective-permute-start | bytes 200 | tf_op jit(solution)/shard_map/ppermute | solution.py:415
  7.0 11.9 %collective-permute-start.1 = (s32[2,8]{1,0:T(2,128)S(1)}, s32[2,8]{1,0:T(2,128)S(1)}, u32[]{:S(2)}, u32[]{:S(2)}) collective-permute-start(s32[2,8]{1,0:T(2,128)S(1)} %pad_add_fusion.pair_ref.refs_0_), channel_id=1, source_target_pairs={{0,2},{1,3},{2,0},{3,1},{4,6},{5,7},{6,4},{7,5},{8,10},{9,11},{10,... | collective-permute-start | bytes 200 | tf_op jit(solution)/shard_map/ppermute | solution.py:415
